TPU v7x, 256 devices: a whole 4x4x8 slice. The times are simulated.
256 devices in a mesh: rows: 128 (over z, y, x), probe: 2 (over core).
Axes of the slice: x: 4, y: 4, z: 8, core: 2. Of those that a mesh axis runs over, the one named last changes fastest.
Arguments:
- probe_matrix: bfloat16 [256, 262144], P('probe', 'rows'), may hold values from -6 to 6
- near_blocks: bfloat16 [1024, 16, 256, 256], P('rows', 'probe'), may hold values from -0.01171875 to 0.01171875
- block_cols: int32 [1024, 16], P('rows', 'probe'), may hold values from 0 to 1023, as said below
Outputs:
- sample: bfloat16 [256, 262144], P('probe', 'rows')
- leaf_factors: float32 [1024, 256, 128], P('rows', 'probe')
- root_factor: float32 [256, 128], P(('rows', 'probe'))
Inputs may be any that keep to these rules, and one draw needn't show every extreme that they name: block_cols[c, 0] = c; every other entry of row c lies within 8 of c; away from the first and last 8 clusters it differs from c; entries are reflected at the ends of the fault and may repeat, or equal c, in rows within 8 of either end.
All inputs are finite; a program needn't handle non-finite values.
Results may differ from a plain program's by a relative error of at most 0.00175.
Values may be sent and summed in bfloat16 or wider, within the bound.
A program may use at most 128 MiB of HBM per device.

v0:
```python
import jax
import jax.numpy as jnp
from jax import lax
from jax.sharding import PartitionSpec as P

K = 128
WIN = 8


def with_halo(block, sides, width):
    for axis, dim in sides:
        count = lax.axis_size(axis)
        forward = [(i, i + 1) for i in range(count - 1)]
        backward = [(target, source) for source, target in forward]
        low = lax.ppermute(
            lax.slice_in_dim(block, block.shape[dim] - width, None, axis=dim), axis, forward
        )
        high = lax.ppermute(lax.slice_in_dim(block, 0, width, axis=dim), axis, backward)
        block = jnp.concatenate([low, block, high], axis=dim)
    return block


def swapped(block, axis, bit):
    count = lax.axis_size(axis)
    route = []
    for low in range(count):
        high = low | 1 << bit
        if high != low and high < count:
            route += [(low, high), (high, low)]
    return lax.ppermute(block, axis, route)


def cross_gram(stacked):
    head_rows = stacked[:, :K, :]
    return jnp.einsum("nkr,npr->nkp", head_rows, stacked, precision=lax.Precision.HIGHEST)


def finish(gram_cross):
    lower_tri = jnp.linalg.cholesky(gram_cross[:, :, :K])
    factor = jax.scipy.linalg.solve_triangular(lower_tri, gram_cross, lower=True)
    return jnp.swapaxes(factor, 1, 2)


def compress(stacked):
    return finish(cross_gram(stacked))


def side_by_side(pieces):
    count = pieces.shape[0]
    return jnp.swapaxes(pieces, 0, 1).reshape(1, pieces.shape[1], count * pieces.shape[2])


def local(probe_matrix, near_blocks, block_cols):
    clusters_dev = near_blocks.shape[0]
    leaf_rows = near_blocks.shape[2]
    columns_dev = probe_matrix.shape[0]
    extended = with_halo(probe_matrix, (("rows", 1),), WIN * leaf_rows)
    local_cols = block_cols - (lax.axis_index("rows") * clusters_dev - WIN)
    rows_piece = lax.all_gather(extended, "probe", axis=0, tiled=True)
    tile_rows = rows_piece.reshape(rows_piece.shape[0], -1, leaf_rows)
    picked_tiles = jnp.take(tile_rows, local_cols, axis=1)
    partial_sample = jnp.einsum(
        "cnij,pcnj->cpi", near_blocks, picked_tiles, preferred_element_type=jnp.float32
    )
    own_part = lax.psum_scatter(partial_sample, "probe", scatter_dimension=1, tiled=True)
    full_sample = lax.all_gather(own_part, "probe", axis=1, tiled=True)
    sample = (
        jnp.swapaxes(own_part, 0, 1)
        .reshape(columns_dev, clusters_dev * leaf_rows)
        .astype(jnp.bfloat16)
    )
    leaf_grams = cross_gram(full_sample)
    leaf_factors = finish(leaf_grams)
    leaf_out = lax.dynamic_slice_in_dim(
        leaf_factors, lax.axis_index("probe") * columns_dev, columns_dev, 1
    )
    node = compress(side_by_side(full_sample))
    for level_bit in range(lax.axis_size("rows").bit_length() - 1):
        partner = swapped(node, "rows", level_bit)
        upper_half = lax.axis_index("rows") >> level_bit & 1 == 1
        first_child = jnp.where(upper_half, partner, node)
        second_child = jnp.where(upper_half, node, partner)
        node = compress(jnp.concatenate([first_child, second_child], axis=-1))
    share_rows = node.shape[1] // (lax.axis_size("rows") * lax.axis_size("probe"))
    device_slot = lax.axis_index("rows") * lax.axis_size("probe") + lax.axis_index("probe")
    root_out = lax.dynamic_slice_in_dim(node[0], device_slot * share_rows, share_rows, 0)
    return (sample, leaf_out, root_out)


def solution(mesh):
    placed = (P("probe", "rows"), P("rows", "probe", None, None), P("rows", "probe"))
    return jax.shard_map(
        local,
        mesh=mesh,
        in_specs=placed,
        out_specs=(P("probe", "rows"), P("rows", "probe", None), P(("rows", "probe"), None)),
        check_vma=False,
    )
```

profile of v0, /device:TPU:1, one launch (start us, length us, event | category | flops | bytes accessed | tf_op | source)
XLA Modules:
  0.0 517.4 jit_solution(12648315295779526735)
XLA Ops:
  7.2 1.3 copy.79
  8.6 4.0 collective-permute-start
  12.5 1.3 collective-permute-start.1
  13.8 9.2 %collective-permute-done = bf16[128,2048]{0,1:T(8,128)(2,1)S(1)} collective-permute-done((bf16[128,2048]{0,1:T(8,128)(2,1)S(1)}, bf16[128,2048]{0,1:T(8,128)(2,1)S(1)}, u32[]{:S(2)}, u32[]{:S(2)}) %collective-permute-start) | collective-permute-done | bytes 524320 | tf_op jit(solution)/shard_map/ppermute | solution.py:15
  23.1 3.8 collective-permute-done.1
  26.9 1.2 pad_maximum_fusion
  28.3 25.5 %all-gather.3.cloned.1.call-done = bf16[256,6144]{0,1:T(8,128)(2,1)} async-done(((bf16[128,6144]{0,1:T(8,128)(2,1)}), bf16[256,6144]{0,1:T(8,128)(2,1)}) %all-gather.3.cloned.1.call-update) | async-done | bytes 3145744 | tf_op jit(solution)/shard_map/all_gather | solution.py:59
  53.8 3.2 copy.82
  57.0 5.5 %gather_fusion = bf16[64,256,256]{2,1,0:T(8,128)(2,1)} fusion(bf16[256,24,256]{2,0,1:T(8,128)(2,1)S(1)} %copy.82, s32[1024]{0:T(1024)S(1)} %pad_clamp_fusion), kind=kCustom, calls=%fused_computation | custom fusion | bytes 16777472 | tf_op jit(solution)/shard_map/jit(_take)/gather | solution.py:61
  62.5 9.5 %fusion.5 = f32[8,256,256]{2,1,0:T(8,128)} fusion(bf16[8,8,256,256]{3,2,1,0:T(8,128)(2,1)} %param.7, bf16[8,8,256,256]{3,2,1,0:T(8,128)(2,1)} %bitcast.180, pred[8,8]{1,0:T(8,128)(4,1)S(1)} %get-tuple-element.14), kind=kOutput, calls=%fused_computation.6 | convolution fusion | flops 2151677952 | bytes 18874432 | tf_op jit(solution)/shard_map/cnij,pcnj->cpi/dot_general | solution.py:62
  72.6 15.7 %reduce-scatter.2.cloned.1.call-done = f32[8,128,256]{2,1,0:T(8,128)} async-done(((f32[8,256,256]{2,1,0:T(8,128)}), f32[8,128,256]{2,1,0:T(8,128)}) %reduce-scatter.2.cloned.1.call-update) | async-done | bytes 1048592 | tf_op jit(solution)/shard_map/reduce_scatter | solution.py:65
  88.4 19.3 %all-gather.5.cloned.1.call-done = f32[8,256,256]{2,1,0:T(8,128)} async-done(((f32[8,128,256]{2,1,0:T(8,128)}), f32[8,256,256]{2,1,0:T(8,128)}) %all-gather.5.cloned.1.call-update) | async-done | bytes 2097168 | tf_op jit(solution)/shard_map/all_gather | solution.py:66
  107.7 1.9 copy.88
  109.6 3.4 fusion.8
  113.2 11.7 %custom-call.30 = f32[1,128,128]{2,1,0:T(8,128)S(1)} custom-call(f32[1,128,128]{2,1,0:T(8,128)S(1)} %fusion.71), custom_call_target="Cholesky" | custom-call | tf_op jit(solution)/shard_map/jit(cholesky)/cholesky | solution.py:39
  124.9 0.6 compare_reduce_fusion.8
  125.5 0.7 select_select_fusion.7
  126.2 9.8 %custom-call.31 = f32[1,128,128]{1,2,0:T(8,128)S(1)} custom-call(f32[1,128,128]{2,1,0:T(8,128)S(1)} %select_select_fusion.7), custom_call_target="InvertDiagBlocksLowerTriangular" | custom-call | tf_op jit(solution)/shard_map/jit(_solve_triangular)/triangular_solve | solution.py:40
  136.3 1.2 collective-permute-start.2
  137.6 3.9 collective-permute-done.2
  142.3 11.7 %custom-call.32 = f32[1,128,128]{2,1,0:T(8,128)S(1)} custom-call(f32[1,128,128]{2,1,0:T(8,128)S(1)} %fusion.69), custom_call_target="Cholesky" | custom-call | tf_op jit(solution)/shard_map/jit(cholesky)/cholesky | solution.py:39
  154.0 0.6 compare_reduce_fusion.7
  154.6 0.8 select_select_fusion.6
  155.5 9.8 %custom-call.33 = f32[1,128,128]{1,2,0:T(8,128)S(1)} custom-call(f32[1,128,128]{2,1,0:T(8,128)S(1)} %select_select_fusion.6), custom_call_target="InvertDiagBlocksLowerTriangular" | custom-call | tf_op jit(solution)/shard_map/jit(_solve_triangular)/triangular_solve | solution.py:40
  165.6 2.7 collective-permute-start.3
  168.3 0.8 convert_bitcast_fusion
  169.2 1.3 copy.83
  170.5 1.0 copy.106
  172.3 11.7 %custom-call.34 = f32[1,128,128]{2,1,0:T(8,128)S(1)} custom-call(f32[1,128,128]{2,1,0:T(8,128)S(1)} %fusion.67), custom_call_target="Cholesky" | custom-call | tf_op jit(solution)/shard_map/jit(cholesky)/cholesky | solution.py:39
  184.0 0.6 compare_reduce_fusion.6
  184.6 0.7 select_select_fusion.5
  185.3 9.8 %custom-call.35 = f32[1,128,128]{1,2,0:T(8,128)S(1)} custom-call(f32[1,128,128]{2,1,0:T(8,128)S(1)} %select_select_fusion.5), custom_call_target="InvertDiagBlocksLowerTriangular" | custom-call | tf_op jit(solution)/shard_map/jit(_solve_triangular)/triangular_solve | solution.py:40
  195.4 1.5 collective-permute-start.4
  197.0 1.9 fusion.9
  200.3 11.7 %custom-call.36 = f32[1,128,128]{2,1,0:T(8,128)S(1)} custom-call(f32[1,128,128]{2,1,0:T(8,128)S(1)} %fusion.65), custom_call_target="Cholesky" | custom-call | tf_op jit(solution)/shard_map/jit(cholesky)/cholesky | solution.py:39
  212.1 0.6 compare_reduce_fusion.5
  212.7 0.7 select_select_fusion.4
  213.4 9.8 %custom-call.37 = f32[1,128,128]{1,2,0:T(8,128)S(1)} custom-call(f32[1,128,128]{2,1,0:T(8,128)S(1)} %select_select_fusion.4), custom_call_target="InvertDiagBlocksLowerTriangular" | custom-call | tf_op jit(solution)/shard_map/jit(_solve_triangular)/triangular_solve | solution.py:40
  223.5 3.3 collective-permute-start.5
  226.9 93.8 %custom-call.14 = f32[8,128,128]{2,1,0:T(8,128)S(1)} custom-call(f32[8,128,128]{2,1,0:T(8,128)S(1)} %fusion.13), custom_call_target="Cholesky" | custom-call | tf_op jit(solution)/shard_map/jit(cholesky)/cholesky | solution.py:39
  321.4 11.7 %custom-call.38 = f32[1,128,128]{2,1,0:T(8,128)S(1)} custom-call(f32[1,128,128]{2,1,0:T(8,128)S(1)} %fusion.63), custom_call_target="Cholesky" | custom-call | tf_op jit(solution)/shard_map/jit(cholesky)/cholesky | solution.py:39
  333.2 0.6 compare_reduce_fusion.4
  333.8 0.7 select_select_fusion.3
  334.5 9.8 %custom-call.39 = f32[1,128,128]{1,2,0:T(8,128)S(1)} custom-call(f32[1,128,128]{2,1,0:T(8,128)S(1)} %select_select_fusion.3), custom_call_target="InvertDiagBlocksLowerTriangular" | custom-call | tf_op jit(solution)/shard_map/jit(_solve_triangular)/triangular_solve | solution.py:40
  344.6 1.5 collective-permute-start.6
  346.3 2.4 collective-permute-done.6
  349.4 11.7 %custom-call.40 = f32[1,128,128]{2,1,0:T(8,128)S(1)} custom-call(f32[1,128,128]{2,1,0:T(8,128)S(1)} %fusion.61), custom_call_target="Cholesky" | custom-call | tf_op jit(solution)/shard_map/jit(cholesky)/cholesky | solution.py:39
  361.2 0.6 compare_reduce_fusion.3
  361.8 0.7 select_select_fusion.2
  362.5 9.8 %custom-call.41 = f32[1,128,128]{1,2,0:T(8,128)S(1)} custom-call(f32[1,128,128]{2,1,0:T(8,128)S(1)} %select_select_fusion.2), custom_call_target="InvertDiagBlocksLowerTriangular" | custom-call | tf_op jit(solution)/shard_map/jit(_solve_triangular)/triangular_solve | solution.py:40
  372.6 2.6 collective-permute-start.7
  375.3 78.6 %custom-call.15 = f32[8,1,128,128]{2,3,1,0:T(8,128)S(1)} custom-call(f32[8,1,128,128]{3,2,1,0:T(8,128)S(1)} %select_bitcast_fusion), custom_call_target="InvertDiagBlocksLowerTriangular" | custom-call | tf_op jit(solution)/shard_map/jit(_solve_triangular)/vmap()/triangular_solve | solution.py:40
  454.7 11.7 %custom-call.42 = f32[1,128,128]{2,1,0:T(8,128)S(1)} custom-call(f32[1,128,128]{2,1,0:T(8,128)S(1)} %fusion.59), custom_call_target="Cholesky" | custom-call | tf_op jit(solution)/shard_map/jit(cholesky)/cholesky | solution.py:39
  466.5 0.6 compare_reduce_fusion.2
  467.1 0.7 select_select_fusion.1
  467.8 9.8 %custom-call.43 = f32[1,128,128]{1,2,0:T(8,128)S(1)} custom-call(f32[1,128,128]{2,1,0:T(8,128)S(1)} %select_select_fusion.1), custom_call_target="InvertDiagBlocksLowerTriangular" | custom-call | tf_op jit(solution)/shard_map/jit(_solve_triangular)/triangular_solve | solution.py:40
  477.9 4.0 collective-permute-start.8
  481.9 1.1 fusion.11
  483.0 0.8 constant_dynamic-slice_fusion
  483.8 2.2 collective-permute-done.8
  486.7 11.7 %custom-call.44 = f32[1,128,128]{2,1,0:T(8,128)S(1)} custom-call(f32[1,128,128]{2,1,0:T(8,128)S(1)} %fusion.57), custom_call_target="Cholesky" | custom-call | tf_op jit(solution)/shard_map/jit(cholesky)/cholesky | solution.py:39
  499.1 0.7 select_select_fusion
  499.8 9.8 %custom-call.45 = f32[1,128,128]{1,2,0:T(8,128)S(1)} custom-call(f32[1,128,128]{2,1,0:T(8,128)S(1)} %select_select_fusion), custom_call_target="InvertDiagBlocksLowerTriangular" | custom-call | tf_op jit(solution)/shard_map/jit(_solve_triangular)/triangular_solve | solution.py:40
  509.9 0.7 dynamic-slice_reduce_fusion
  (82 shorter events, 10.4 us)
Async XLA Ops:
  7.2 21.1 %copy-start.2 = (s32[8,8]{1,0:T(8,128)S(1)}, s32[8,8]{1,0:T(8,128)}, u32[]{:S(2)}) copy-start(s32[8,8]{1,0:T(8,128)} %param.8) | copy-start | bytes 772
  7.2 46.6 %all-gather.3.cloned.1.call-start = ((), (), s32[]{:S(2)}) async-start(), calls=%async_computation.1 | async-start | bytes 4718592 | tf_op jit(solution)/shard_map/all_gather | solution.py:59
  8.6 14.5 %collective-permute-start = (bf16[128,2048]{0,1:T(8,128)(2,1)S(1)}, bf16[128,2048]{0,1:T(8,128)(2,1)S(1)}, u32[]{:S(2)}, u32[]{:S(2)}) collective-permute-start(bf16[128,2048]{0,1:T(8,128)(2,1)S(1)} %copy.79), channel_id=1, source_target_pairs={{0,2},{2,4},{4,6},{6,8},{8,10},{10,12},{12,14},{14,16},{16,18},{18... | collective-permute-start | bytes 1572872 | tf_op jit(solution)/shard_map/ppermute | solution.py:15
  12.5 14.4 %collective-permute-start.1 = (bf16[128,2048]{0,1:T(8,128)(2,1)S(1)}, bf16[128,2048]{0,1:T(8,128)(2,1)S(1)}, u32[]{:S(2)}, u32[]{:S(2)}) collective-permute-start(bf16[128,2048]{0,1:T(8,128)(2,1)S(1)} %copy.79), channel_id=1, source_target_pairs={{2,0},{4,2},{6,4},{8,6},{10,8},{12,10},{14,12},{16,14},{18,16},{20... | collective-permute-start | bytes 1572872 | tf_op jit(solution)/shard_map/ppermute | solution.py:18
  28.2 60.2 %reduce-scatter.2.cloned.1.call-start = ((), (), s32[]{:S(2)}) async-start(), calls=%async_computation.2 | async-start | bytes 3145728 | tf_op jit(solution)/shard_map/reduce_scatter | solution.py:65
  72.1 35.6 %all-gather.5.cloned.1.call-start = ((), (), s32[]{:S(2)}) async-start(), calls=%async_computation.3 | async-start | bytes 3145728 | tf_op jit(solution)/shard_map/all_gather | solution.py:66
  113.0 55.3 %copy-start.1 = (f32[8,128,256]{2,1,0:T(8,128)S(1)}, f32[8,128,256]{2,1,0:T(8,128)}, u32[]{:S(2)}) copy-start(f32[8,128,256]{2,1,0:T(8,128)} %reduce-scatter.2.cloned.1.call-done) | copy-start | bytes 3145732
  136.3 5.2 collective-permute-start.2
  154.6 42.3 %copy-start = (f32[8,256,256]{2,1,0:T(8,128)S(1)}, f32[8,256,256]{2,1,0:T(8,128)}, u32[]{:S(2)}) copy-start(f32[8,256,256]{2,1,0:T(8,128)} %all-gather.5.cloned.1.call-done) | copy-start | bytes 6291460
  165.6 5.9 %collective-permute-start.3 = (f32[1,256,128]{1,2,0:T(8,128)S(1)}, f32[1,256,128]{1,2,0:T(8,128)S(1)}, u32[]{:S(2)}, u32[]{:S(2)}) collective-permute-start(f32[1,256,128]{1,2,0:T(8,128)S(1)} %convolution_bitcast_fusion.6), channel_id=1, source_target_pairs={{0,4},{4,0},{2,6},{6,2},{8,12},{12,8},{10,14},{14,10},{16,20},{20,... | collective-permute-start | bytes 393224 | tf_op jit(solution)/shard_map/ppermute | solution.py:30
  195.4 4.2 collective-permute-start.4
  223.5 97.1 %collective-permute-start.5 = (f32[1,256,128]{1,2,0:T(8,128)S(1)}, f32[1,256,128]{1,2,0:T(8,128)S(1)}, u32[]{:S(2)}, u32[]{:S(2)}) collective-permute-start(f32[1,256,128]{1,2,0:T(8,128)S(1)} %convolution_bitcast_fusion.4), channel_id=1, source_target_pairs={{0,16},{16,0},{2,18},{18,2},{4,20},{20,4},{6,22},{22,6},{8,24},{24... | collective-permute-start | bytes 393224 | tf_op jit(solution)/shard_map/ppermute | solution.py:30
  344.6 4.1 collective-permute-start.6
  372.6 81.3 %collective-permute-start.7 = (f32[1,256,128]{1,2,0:T(8,128)S(1)}, f32[1,256,128]{1,2,0:T(8,128)S(1)}, u32[]{:S(2)}, u32[]{:S(2)}) collective-permute-start(f32[1,256,128]{1,2,0:T(8,128)S(1)} %convolution_bitcast_fusion.2), channel_id=1, source_target_pairs={{0,64},{64,0},{2,66},{66,2},{4,68},{68,4},{6,70},{70,6},{8,72},{72... | collective-permute-start | bytes 393224 | tf_op jit(solution)/shard_map/ppermute | solution.py:30
  477.9 8.1 %collective-permute-start.8 = (f32[1,256,128]{1,2,0:T(8,128)S(1)}, f32[1,256,128]{1,2,0:T(8,128)S(1)}, u32[]{:S(2)}, u32[]{:S(2)}) collective-permute-start(f32[1,256,128]{1,2,0:T(8,128)S(1)} %convolution_bitcast_fusion.1), channel_id=1, source_target_pairs={{0,128},{128,0},{2,130},{130,2},{4,132},{132,4},{6,134},{134,6},{8... | collective-permute-start | bytes 393224 | tf_op jit(solution)/shard_map/ppermute | solution.py:30
Sparse Core Ops, SparseCore 0:
  28.3 25.4 all-gather.2
  72.2 16.1 reduce-scatter.1
  90.3 17.3 all-gather.4
where the time goes:
time: 526 us; the launch traced here: 517 us
  other arithmetic  358 us (68%)
  waiting for transfers between devices  82.5 us (16%)
  starting transfers between devices  22.7 us (4%)
  matrix products  22.6 us (4%)
  local copies, waits for them, and re-layouts  16.9 us (3%)
  between operations  14.7 us (3%)
    another operation x28, other arithmetic, finish(): lower_tri = jnp.linalg.cholesky(gram_cross[:, :, :K])  193 us
    another operation x19, other arithmetic, finish(): jax.scipy.linalg.solve_triangular(lower_tri, gram_cross, lower=True)  163 us
    all_gather x1, waiting for transfers between devices, local(): rows_piece = lax.all_gather(extended, 'probe', axis=0, tiled=True)  25.5 us
    all_gather x1, waiting for transfers between devices, local(): full_sample = lax.all_gather(own_part, 'probe', axis=1, tiled=True)  19.3 us
    ppermute x7, starting transfers between devices, swapped(): return lax.ppermute(block, axis, route)  16.8 us
    reduce_scatter x1, waiting for transfers between devices, local(): lax.psum_scatter(partial_sample, 'probe', scatter_dimension=1, tiled=True)  15.7 us
  transfers between devices with their start and end apart: 12, of which 9 were waited for; matrix products, arithmetic and copies ran while one was open for 35% of the time, Pallas kernels for 0%

commit v1 on v0

v1 whole, which is shorter than its diff:
```python
import functools

import jax
import jax.numpy as jnp
from jax import lax
from jax.experimental import pallas as pl
from jax.experimental.pallas import tpu as pltpu
from jax.sharding import PartitionSpec as P

K = 128
WIN = 8


def with_halo(block, sides, width):
    for axis, dim in sides:
        count = lax.axis_size(axis)
        forward = [(i, i + 1) for i in range(count - 1)]
        backward = [(target, source) for source, target in forward]
        low = lax.ppermute(
            lax.slice_in_dim(block, block.shape[dim] - width, None, axis=dim), axis, forward
        )
        high = lax.ppermute(lax.slice_in_dim(block, 0, width, axis=dim), axis, backward)
        block = jnp.concatenate([low, block, high], axis=dim)
    return block


def cross_gram(stacked):
    head_rows = stacked[:, :K, :]
    return jnp.einsum("nkr,npr->nkp", head_rows, stacked, precision=lax.Precision.HIGHEST)


def eliminate_panel(groups, first, ncols):
    ng=len(groups)
    iota=lax.broadcasted_iota(jnp.int32,(8,K),0)
    W=groups[0].shape[1]
    nh=W//K
    G=[[g[:,h*K:(h+1)*K] for h in range(nh)] for g in groups]
    for j in range(8*ng):
        c=first+j; gj,sj=divmod(j,8)
        bc=jnp.broadcast_to(G[gj][0][:,c:c+1],(8,K))
        inv=1.0/bc[sj:sj+1,:]
        rows=[G[gj][h][sj:sj+1,:]*inv for h in range(nh)]
        for g in range(gj,ng):
            if g==gj:
                if sj==7: continue
                m=jnp.where(iota>sj,bc,0.0)
            else:
                m=jnp.broadcast_to(G[g][0][:,c:c+1],(8,K))
            for h in range(nh):
                G[g][h]=G[g][h]-m*rows[h]
    return G
def factor_many(a_ref, ms, b, W=2*K):
    ng=b//8
    lane=lax.broadcasted_iota(jnp.int32,(8,K),1)
    sub=lax.broadcasted_iota(jnp.int32,(8,K),0)
    for k in range(K//b):
        outs=[]
        for m in ms:
            P=[a_ref[m,k*b+8*g:k*b+8*g+8,:] for g in range(ng)]
            outs.append(P)
        res=[eliminate_panel(P,k*b,b) for P in outs]
        for m,G in zip(ms,res):
            full=[]
            for g in range(ng):
                r0=k*b+8*g
                d=jnp.sum(jnp.where(lane==r0+sub,G[g][0],0.0),axis=1,keepdims=True)
                rs=lax.rsqrt(d)
                G[g][0]=jnp.where(lane>=r0+sub,G[g][0]*rs,0.0)
                for h in range(1,len(G[g])): G[g][h]=G[g][h]*rs
                row=jnp.concatenate(G[g],axis=1)
                a_ref[m,r0:r0+8,:]=row
                full.append(row)
            if (k+1)*b<K:
                R=jnp.concatenate(full,axis=0)
                left=R[:,:K].T[(k+1)*b:,:]
                a_ref[m,(k+1)*b:,:]=a_ref[m,(k+1)*b:,:]-jnp.dot(left,R,precision=lax.Precision.HIGHEST,preferred_element_type=jnp.float32)
def kernel(c_ref,o_ref,a_ref,*,b,groups):
    a_ref[...]=c_ref[...]
    for ms in groups:
        factor_many(a_ref,ms,b)
    for m in range(c_ref.shape[0]):
        o_ref[m]=a_ref[m].T
def call(c,b,groups):
    nb=c.shape[0]
    return pl.pallas_call(functools.partial(kernel,b=b,groups=groups),
      out_shape=jax.ShapeDtypeStruct((nb,2*K,K),jnp.float32),
      in_specs=[pl.BlockSpec(memory_space=pltpu.VMEM)],out_specs=pl.BlockSpec(memory_space=pltpu.VMEM),
      scratch_shapes=[pltpu.VMEM((nb,K,2*K),jnp.float32)],
      name="factor")(c)
def local(probe_matrix, near_blocks, block_cols):
    clusters_dev = near_blocks.shape[0]
    leaf_rows = near_blocks.shape[2]
    columns_dev = probe_matrix.shape[0]
    extended = with_halo(probe_matrix, (("rows", 1),), WIN * leaf_rows)
    local_cols = block_cols - (lax.axis_index("rows") * clusters_dev - WIN)
    rows_piece = lax.all_gather(extended, "probe", axis=0, tiled=True)
    tile_rows = rows_piece.reshape(rows_piece.shape[0], -1, leaf_rows)
    picked_tiles = jnp.take(tile_rows, local_cols, axis=1)
    partial_sample = jnp.einsum(
        "cnij,pcnj->cpi", near_blocks, picked_tiles, preferred_element_type=jnp.float32
    )
    own_part = lax.psum_scatter(partial_sample, "probe", scatter_dimension=1, tiled=True)
    full_sample = lax.all_gather(own_part, "probe", axis=1, tiled=True)
    sample = (
        jnp.swapaxes(own_part, 0, 1)
        .reshape(columns_dev, clusters_dev * leaf_rows)
        .astype(jnp.bfloat16)
    )
    leaf_grams = cross_gram(full_sample)
    root_gram = lax.psum(jnp.sum(leaf_grams, axis=0), "rows")
    factors = call(jnp.concatenate([leaf_grams, root_gram[None]], axis=0), 16, [list(range(clusters_dev + 1))])
    leaf_out = lax.dynamic_slice_in_dim(
        factors[:clusters_dev], lax.axis_index("probe") * columns_dev, columns_dev, 1
    )
    root = factors[clusters_dev]
    share_rows = root.shape[0] // (lax.axis_size("rows") * lax.axis_size("probe"))
    device_slot = lax.axis_index("rows") * lax.axis_size("probe") + lax.axis_index("probe")
    root_out = lax.dynamic_slice_in_dim(root, device_slot * share_rows, share_rows, 0)
    return (sample, leaf_out, root_out)


def solution(mesh):
    placed = (P("probe", "rows"), P("rows", "probe", None, None), P("rows", "probe"))
    return jax.shard_map(
        local,
        mesh=mesh,
        in_specs=placed,
        out_specs=(P("probe", "rows"), P("rows", "probe", None), P(("rows", "probe"), None)),
        check_vma=False,
    )
```

time: 526 us -> 359 us (0.68)
  other arithmetic: 358 us -> 3.37 us
  waiting for transfers between devices: 82.5 us -> 281 us
  Pallas kernels: 0 us -> 22 us
  starting transfers between devices: 22.7 us -> 6.24 us
  matrix products: 22.6 us -> 14.3 us
    another operation x47 -> x0, other arithmetic: 356 us -> none  [the longest x28 193 us: finish(): lower_tri = jnp.linalg.cholesky(gram_cross[:, :, :K])]
    psum x0 -> x1, waiting for transfers between devices: none -> 208 us  [local(): root_gram = lax.psum(jnp.sum(leaf_grams, axis=0), 'rows')]
    pallas_call x0 -> x1, Pallas kernels: none -> 22 us  [call(): pl.pallas_call(functools.partial(kernel, b=b, groups=groups), out_shape=j...]
    ppermute x7 -> x0, starting transfers between devices: 16.8 us -> none  [swapped(): return lax.ppermute(block, axis, route)]
    ppermute x7 -> x0, waiting for transfers between devices: 8.9 us -> none  [swapped(): return lax.ppermute(block, axis, route)]
    ppermute x1, waiting for transfers between devices: 9.24 us -> 0.9 us  [with_halo(): lax.ppermute(lax.slice_in_dim(block, block.shape[dim] - width, None, axis...]
  transfers between devices with their start and end apart: 12 -> 6, of which waited for: 9 -> 6; matrix products, arithmetic and copies ran while one was open for 35% -> 0% of each run, Pallas kernels for 0% -> 0%
where the time goes in v1:
time: 359 us; the launch traced here: 355 us
  waiting for transfers between devices  281 us (78%)
  Pallas kernels  22 us (6%)
  matrix products  14.3 us (4%)
  local copies, waits for them, and re-layouts  14 us (4%)
  between operations  13.9 us (4%)
  starting transfers between devices  6.24 us (2%)
    psum x1, waiting for transfers between devices, local(): root_gram = lax.psum(jnp.sum(leaf_grams, axis=0), 'rows')  208 us
    all_gather x1, waiting for transfers between devices, local(): rows_piece = lax.all_gather(extended, 'probe', axis=0, tiled=True)  29.6 us
    pallas_call x1, Pallas kernels, call(): pl.pallas_call(functools.partial(kernel, b=b, groups=groups), out_shape=j...  22 us
    all_gather x1, waiting for transfers between devices, local(): full_sample = lax.all_gather(own_part, 'probe', axis=1, tiled=True)  19.1 us
    reduce_scatter x1, waiting for transfers between devices, local(): lax.psum_scatter(partial_sample, 'probe', scatter_dimension=1, tiled=True)  16.2 us
    dot_general x1, matrix products, local(): jnp.einsum('cnij,pcnj->cpi', near_blocks, picked_tiles, preferred_element...  9.51 us
    ppermute x1, waiting for transfers between devices, with_halo(): lax.ppermute(lax.slice_in_dim(block, 0, width, axis=dim), axis, backward)  7.33 us
  transfers between devices with their start and end apart: 6, of which 6 were waited for; matrix products, arithmetic and copies ran while one was open for 0% of the time, Pallas kernels for 0%

profile of v1, /device:TPU:1, one launch (start us, length us, event | category | flops | bytes accessed | tf_op | source)
XLA Modules:
  0.0 355.2 jit_solution(6488929082766275029)
XLA Ops:
  7.2 0.0 copy-start.1
  7.2 0.0 all-gather.3.cloned.1.call-start
  7.2 1.3 copy.9
  8.5 1.3 collective-permute-start.1
  9.8 4.6 %collective-permute-start = (bf16[128,2048]{0,1:T(8,128)(2,1)S(1)}, bf16[128,2048]{0,1:T(8,128)(2,1)S(1)}, u32[]{:S(2)}, u32[]{:S(2)}) collective-permute-start(bf16[128,2048]{0,1:T(8,128)(2,1)S(1)} %copy.9), channel_id=1, source_target_pairs={{0,2},{2,4},{4,6},{6,8},{8,10},{10,12},{12,14},{14,16},{16,18},{18... | collective-permute-start | bytes 1572872 | tf_op jit(solution)/shard_map/ppermute | solution.py:19
  14.4 7.3 %collective-permute-done.1 = bf16[128,2048]{0,1:T(8,128)(2,1)S(1)} collective-permute-done((bf16[128,2048]{0,1:T(8,128)(2,1)S(1)}, bf16[128,2048]{0,1:T(8,128)(2,1)S(1)}, u32[]{:S(2)}, u32[]{:S(2)}) %collective-permute-start.1) | collective-permute-done | bytes 524320 | tf_op jit(solution)/shard_map/ppermute | solution.py:22
  21.8 0.9 collective-permute-done
  22.7 1.3 pad_maximum_fusion
  23.9 0.0 all-gather.3.cloned.1.call-update
  24.0 0.0 reduce-scatter.2.cloned.1.call-start
  24.0 0.0 copy-done.1
  24.0 0.1 reshape.20
  24.1 29.6 %all-gather.3.cloned.1.call-done = bf16[256,6144]{0,1:T(8,128)(2,1)} async-done(((bf16[128,6144]{0,1:T(8,128)(2,1)}), bf16[256,6144]{0,1:T(8,128)(2,1)}) %all-gather.3.cloned.1.call-update) | async-done | bytes 3145744 | tf_op jit(solution)/shard_map/all_gather | solution.py:96
  53.8 3.2 copy.12
  56.9 5.5 %gather_fusion = bf16[64,256,256]{2,1,0:T(8,128)(2,1)} fusion(bf16[256,24,256]{2,0,1:T(8,128)(2,1)S(1)} %copy.12, s32[1024]{0:T(1024)S(1)} %pad_clamp_fusion), kind=kCustom, calls=%fused_computation | custom fusion | bytes 16777472 | tf_op jit(solution)/shard_map/jit(_take)/gather | solution.py:98
  62.5 9.5 %fusion.5 = f32[8,256,256]{2,1,0:T(8,128)} fusion(bf16[8,8,256,256]{3,2,1,0:T(8,128)(2,1)} %param.4, bf16[8,8,256,256]{3,2,1,0:T(8,128)(2,1)} %bitcast.18, pred[8,8]{1,0:T(8,128)(4,1)S(1)} %get-tuple-element.9), kind=kOutput, calls=%fused_computation.6 | convolution fusion | flops 2151677952 | bytes 18874432 | tf_op jit(solution)/shard_map/cnij,pcnj->cpi/dot_general | solution.py:99
  72.0 0.0 reduce-scatter.2.cloned.1.call-update
  72.0 0.0 all-gather.5.cloned.1.call-start
  72.0 16.2 %reduce-scatter.2.cloned.1.call-done = f32[8,128,256]{2,1,0:T(8,128)} async-done(((f32[8,256,256]{2,1,0:T(8,128)}), f32[8,128,256]{2,1,0:T(8,128)}) %reduce-scatter.2.cloned.1.call-update) | async-done | bytes 1048592 | tf_op jit(solution)/shard_map/reduce_scatter | solution.py:102
  88.3 0.0 copy-start
  88.3 0.0 all-gather.5.cloned.1.call-update
  88.3 0.2 all-reduce.2.cloned.1.call-start
  88.6 19.1 %all-gather.5.cloned.1.call-done = f32[8,256,256]{2,1,0:T(8,128)} async-done(((f32[8,128,256]{2,1,0:T(8,128)}), f32[8,256,256]{2,1,0:T(8,128)}) %all-gather.5.cloned.1.call-update) | async-done | bytes 2097168 | tf_op jit(solution)/shard_map/all_gather | solution.py:103
  107.6 4.8 %fusion.11 = (f32[128,256]{1,0:T(8,128)}, f32[8,128,256]{2,1,0:T(8,128)S(1)}) fusion(f32[8,256,256]{2,1,0:T(8,128)} %all-gather.5.cloned.1.call-done), kind=kOutput, calls=%fused_computation.18 | convolution fusion | flops 805535744 | bytes 4325376 | tf_op jit(solution)/shard_map/nkr,npr->nkp/dot_general | solution.py:29
  112.4 0.0 all-reduce.2.cloned.1.call-update
  112.4 0.0 copy-done
  112.4 0.1 convert_bitcast_fusion
  112.5 0.3 copy.13
  112.8 1.0 copy.14
  113.8 208.2 %all-reduce.2.cloned.1.call-done = f32[1,128,256]{2,1,0:T(8,128)} async-done(((f32[1,128,256]{2,1,0:T(8,128)}), f32[1,128,256]{2,1,0:T(8,128)}) %all-reduce.2.cloned.1.call-update) | async-done | bytes 131088 | tf_op jit(solution)/shard_map/psum | solution.py:110
  322.0 2.0 pad_maximum_fusion.1.c_ref
  324.0 22.0 %factor.1 = f32[9,256,128]{2,1,0:T(8,128)} custom-call(f32[9,128,256]{2,1,0:T(8,128)} %pad_maximum_fusion.1.c_ref), custom_call_target="tpu_custom_call" | custom-call | tf_op jit(solution)/shard_map/factor/pallas_call | solution.py:85
  346.0 0.0 slice-start
  346.0 1.3 slice.15
  347.3 0.8 constant_dynamic-slice_fusion
  348.1 0.0 slice-done
  348.1 0.5 dynamic-slice_bitcast_fusion
  (2 shorter events, 0.0 us)
Async XLA Ops:
  7.2 16.9 %copy-start.1 = (s32[8,8]{1,0:T(8,128)S(1)}, s32[8,8]{1,0:T(8,128)}, u32[]{:S(2)}) copy-start(s32[8,8]{1,0:T(8,128)} %param.5) | copy-start | bytes 772
  7.2 46.6 %all-gather.3.cloned.1.call-start = ((), (), s32[]{:S(2)}) async-start(), calls=%async_computation.1 | async-start | bytes 4718592 | tf_op jit(solution)/shard_map/all_gather | solution.py:96
  8.5 13.2 %collective-permute-start.1 = (bf16[128,2048]{0,1:T(8,128)(2,1)S(1)}, bf16[128,2048]{0,1:T(8,128)(2,1)S(1)}, u32[]{:S(2)}, u32[]{:S(2)}) collective-permute-start(bf16[128,2048]{0,1:T(8,128)(2,1)S(1)} %copy.9), channel_id=1, source_target_pairs={{2,0},{4,2},{6,4},{8,6},{10,8},{12,10},{14,12},{16,14},{18,16},{20... | collective-permute-start | bytes 1572872 | tf_op jit(solution)/shard_map/ppermute | solution.py:22
  9.8 12.8 %collective-permute-start = (bf16[128,2048]{0,1:T(8,128)(2,1)S(1)}, bf16[128,2048]{0,1:T(8,128)(2,1)S(1)}, u32[]{:S(2)}, u32[]{:S(2)}) collective-permute-start(bf16[128,2048]{0,1:T(8,128)(2,1)S(1)} %copy.9), channel_id=1, source_target_pairs={{0,2},{2,4},{4,6},{6,8},{8,10},{10,12},{12,14},{14,16},{16,18},{18... | collective-permute-start | bytes 1572872 | tf_op jit(solution)/shard_map/ppermute | solution.py:19
  24.0 64.3 %reduce-scatter.2.cloned.1.call-start = ((), (), s32[]{:S(2)}) async-start(), calls=%async_computation.2 | async-start | bytes 3145728 | tf_op jit(solution)/shard_map/reduce_scatter | solution.py:102
  72.0 35.6 %all-gather.5.cloned.1.call-start = ((), (), s32[]{:S(2)}) async-start(), calls=%async_computation.3 | async-start | bytes 3145728 | tf_op jit(solution)/shard_map/all_gather | solution.py:103
  88.3 24.1 %copy-start = (f32[8,128,256]{2,1,0:T(8,128)S(1)}, f32[8,128,256]{2,1,0:T(8,128)}, u32[]{:S(2)}) copy-start(f32[8,128,256]{2,1,0:T(8,128)} %reduce-scatter.2.cloned.1.call-done) | copy-start | bytes 3145732
  88.3 233.7 %all-reduce.2.cloned.1.call-start = ((), (), s32[]{:S(2)}) async-start(), calls=%async_computation.4 | async-start | bytes 262144 | tf_op jit(solution)/shard_map/psum | solution.py:110
  346.0 2.2 slice-start
Sparse Core Ops, SparseCore 0:
  24.1 29.6 all-gather.2
  72.1 16.1 reduce-scatter.1
  90.2 17.3 all-gather.4
  114.3 207.5 all-reduce.1

commit v2 on v1

v2 whole, which is shorter than its diff:
```python
import functools

import jax
import jax.numpy as jnp
from jax import lax
from jax.experimental import pallas as pl
from jax.experimental.pallas import tpu as pltpu
from jax.sharding import PartitionSpec as P

K = 128
LEAF = 256
PLANE = 16
HIGH = lax.Precision.HIGHEST
ORDER = (3, 4, 2, 5, 1, 6, 0, 7)


def cross(a, b, precision=None):
    return lax.dot_general(
        a, b, (((1,), (1,)), ((), ())), precision=precision, preferred_element_type=jnp.float32
    )


def gather_kernel(
    depth, cols_ref, probe_ref, blocks_ref,
    sample_ref, grams_ref, root_ref,
    own, landing, window, blocks, mine, theirs, total, rs_buf, z_buf,
    block_sem, own_sem, share_send, share_recv, halo_send, halo_recv, pass_send, pass_recv,
    part_send, part_recv, rs_send, rs_recv, z_send, z_recv, ag_send, ag_recv,
):
    row, core = lax.axis_index("rows"), lax.axis_index("probe")
    rows = PLANE * depth
    sibling = (row, 1 - core)
    after, before = (lax.rem(row + 1, rows), core), (lax.rem(row + rows - 1, rows), core)
    layer, spot = row // PLANE, lax.rem(row, PLANE)

    def in_plane(step):
        return (layer * PLANE + lax.rem(spot + step, PLANE), core)

    def in_column(step):
        return (lax.rem(layer + step, depth) * PLANE + spot, core)

    barrier = pltpu.get_barrier_semaphore()
    for target in (after, before, sibling):
        pl.semaphore_signal(barrier, inc=1, device_id=target, device_id_type=pl.DeviceIdType.MESH)

    def greet_plane(step, carry):
        pl.semaphore_signal(barrier, inc=1, device_id=in_plane(step), device_id_type=pl.DeviceIdType.MESH)
        return carry

    def greet_column(step, carry):
        pl.semaphore_signal(barrier, inc=1, device_id=in_column(step), device_id_type=pl.DeviceIdType.MESH)
        return carry

    lax.fori_loop(1, PLANE, greet_plane, 0)
    lax.fori_loop(1, depth, greet_column, 0)

    own_copy = pltpu.make_async_copy(probe_ref, own.at[core], own_sem)
    own_copy.start()
    block_copies = {}
    for c in ORDER:
        block_copies[c] = pltpu.make_async_copy(blocks_ref.at[c], blocks.at[c], block_sem.at[c])
        block_copies[c].start()
    pl.semaphore_wait(barrier, 3 + PLANE - 1 + depth - 1)

    def remote(src, dst, send, recv, target):
        return pltpu.make_async_remote_copy(
            src_ref=src, dst_ref=dst, send_sem=send, recv_sem=recv,
            device_id=target, device_id_type=pl.DeviceIdType.MESH,
        )

    halo = {}
    for t in range(8):
        for side, c, target in ((0, 7 - t, after), (1, t, before)):
            halo[side, t] = remote(
                probe_ref.at[:, c * LEAF:(c + 1) * LEAF], landing.at[side, c, core],
                halo_send.at[side, c], halo_recv.at[side, c], target,
            )
            halo[side, t].start()
    share = remote(probe_ref, own.at[core], share_send, share_recv, sibling)
    share.start()

    own_copy.wait()
    share.wait_recv()
    for c in range(8):
        for half in range(2):
            window[8 + c, half * K:(half + 1) * K, :] = own[half, :, c * LEAF:(c + 1) * LEAF]

    passed = {}
    parts = {}

    def absorb(t):
        for side, c in ((0, 7 - t), (1, t)):
            passed[side, t].wait_recv()
            for half in range(2):
                window[16 * side + c, half * K:(half + 1) * K, :] = landing[side, c, half]

    def multiply(c):
        block_copies[c].wait()
        acc = jnp.zeros((LEAF, LEAF), jnp.float32)
        for b in range(8):
            at = jnp.clip(cols_ref[c, b] - (row * 8 - 8), 0, 23)
            acc = acc + cross(window[at], blocks[c, b])
        mine[c] = acc
        parts[c] = remote(mine.at[c], theirs.at[c], part_send.at[c], part_recv.at[c], sibling)
        parts[c].start()

    def gram(c, first):
        parts[c].wait_recv()
        full = mine[c] + theirs[c]
        theirs[c] = full
        kept = theirs[c, pl.ds(pl.multiple_of(core * K, K), K), :]
        sample_ref[:, c * LEAF:(c + 1) * LEAF] = kept.astype(jnp.bfloat16)
        g = cross(full[:K], full, HIGH)
        grams_ref[c] = g
        total[...] = g if first else total[...] + g

    for t in range(8):
        for side, c in ((0, 7 - t), (1, t)):
            halo[side, t].wait_recv()
            passed[side, t] = remote(
                landing.at[side, c, core], landing.at[side, c, core],
                pass_send.at[side, c], pass_recv.at[side, c], sibling,
            )
            passed[side, t].start()
        absorb(t)
        if t >= 4:
            for c in (7 - t, t):
                multiply(c)
        if t >= 5:
            for c in (8 - t, t - 1):
                gram(c, c == 3)
    for c in (0, 7):
        gram(c, False)

    def scatter(step, carry):
        at = pl.multiple_of(lax.rem(spot + step, PLANE) * 8, 8)
        remote(total.at[pl.ds(at, 8), :], rs_buf.at[step], rs_send.at[step], rs_recv.at[step], in_plane(step)).start()
        return carry

    def scattered(step, carry):
        remote(total.at[pl.ds(0, 8), :], rs_buf.at[step], rs_send.at[step], rs_recv.at[step], in_plane(step)).wait()
        return carry

    lax.fori_loop(1, PLANE, scatter, 0)
    rs_buf[0] = total[pl.ds(pl.multiple_of(spot * 8, 8), 8), :]
    lax.fori_loop(1, PLANE, scattered, 0)
    z_buf[0] = jnp.sum(rs_buf[...], axis=0)

    def column(step):
        return remote(z_buf.at[0], z_buf.at[step], z_send.at[step], z_recv.at[step], in_column(step))

    def spread(step, carry):
        column(step).start()
        return carry

    def gathered(step, carry):
        column(step).wait()
        return carry

    lax.fori_loop(1, depth, spread, 0)
    lax.fori_loop(1, depth, gathered, 0)
    here = pl.ds(pl.multiple_of(spot * 8, 8), 8)
    root_ref[here, :] = jnp.sum(z_buf[...], axis=0)

    def publish(step):
        return remote(root_ref.at[here, :], root_ref.at[here, :], ag_send.at[step], ag_recv.at[step], in_plane(step))

    def published(step, carry):
        publish(step).start()
        return carry

    def finished(step, carry):
        publish(step).wait_send()
        from_row = pl.ds(pl.multiple_of(lax.rem(spot + PLANE - step, PLANE) * 8, 8), 8)
        remote(root_ref.at[from_row, :], root_ref.at[from_row, :], ag_send.at[step], ag_recv.at[step], in_plane(step)).wait_recv()
        return carry

    lax.fori_loop(1, PLANE, published, 0)
    lax.fori_loop(1, PLANE, finished, 0)

    share.wait_send()
    for copy in list(halo.values()) + list(passed.values()) + list(parts.values()):
        copy.wait_send()


def gather(block_cols, probe_matrix, near_blocks):
    depth = lax.axis_size("rows") // PLANE
    bf16, f32, dma = jnp.bfloat16, jnp.float32, pltpu.SemaphoreType.DMA
    whole = pl.BlockSpec(memory_space=pltpu.VMEM)
    return pl.pallas_call(
        functools.partial(gather_kernel, depth),
        out_shape=(
            jax.ShapeDtypeStruct((K, 8 * LEAF), bf16),
            jax.ShapeDtypeStruct((8, K, LEAF), f32),
            jax.ShapeDtypeStruct((K, LEAF), f32),
        ),
        in_specs=[
            pl.BlockSpec(memory_space=pltpu.SMEM),
            pl.BlockSpec(memory_space=pl.ANY),
            pl.BlockSpec(memory_space=pl.ANY),
        ],
        out_specs=(whole, whole, whole),
        scratch_shapes=[
            pltpu.VMEM((2, K, 8 * LEAF), bf16),
            pltpu.VMEM((2, 8, 2, K, LEAF), bf16),
            pltpu.VMEM((24, LEAF, LEAF), bf16),
            pltpu.VMEM((8, 8, LEAF, LEAF), bf16),
            pltpu.VMEM((8, LEAF, LEAF), f32),
            pltpu.VMEM((8, LEAF, LEAF), f32),
            pltpu.VMEM((K, LEAF), f32),
            pltpu.VMEM((PLANE, 8, LEAF), f32),
            pltpu.VMEM((depth, 8, LEAF), f32),
            dma((8,)), dma, dma, dma, dma((2, 8)), dma((2, 8)), dma((2, 8)), dma((2, 8)),
            dma((8,)), dma((8,)), dma((PLANE,)), dma((PLANE,)),
            dma((depth,)), dma((depth,)), dma((PLANE,)), dma((PLANE,)),
        ],
        compiler_params=pltpu.CompilerParams(
            collective_id=0, has_side_effects=True, vmem_limit_bytes=40 * 2**20
        ),
        name="gather",
    )(block_cols, probe_matrix, near_blocks)


def eliminate_panel(groups, first, ncols):
    ng=len(groups)
    iota=lax.broadcasted_iota(jnp.int32,(8,K),0)
    W=groups[0].shape[1]
    nh=W//K
    G=[[g[:,h*K:(h+1)*K] for h in range(nh)] for g in groups]
    for j in range(8*ng):
        c=first+j; gj,sj=divmod(j,8)
        bc=jnp.broadcast_to(G[gj][0][:,c:c+1],(8,K))
        inv=1.0/bc[sj:sj+1,:]
        rows=[G[gj][h][sj:sj+1,:]*inv for h in range(nh)]
        for g in range(gj,ng):
            if g==gj:
                if sj==7: continue
                m=jnp.where(iota>sj,bc,0.0)
            else:
                m=jnp.broadcast_to(G[g][0][:,c:c+1],(8,K))
            for h in range(nh):
                G[g][h]=G[g][h]-m*rows[h]
    return G
def factor_many(a_ref, ms, b, W=2*K):
    ng=b//8
    lane=lax.broadcasted_iota(jnp.int32,(8,K),1)
    sub=lax.broadcasted_iota(jnp.int32,(8,K),0)
    for k in range(K//b):
        outs=[]
        for m in ms:
            P=[a_ref[m,k*b+8*g:k*b+8*g+8,:] for g in range(ng)]
            outs.append(P)
        res=[eliminate_panel(P,k*b,b) for P in outs]
        for m,G in zip(ms,res):
            full=[]
            for g in range(ng):
                r0=k*b+8*g
                d=jnp.sum(jnp.where(lane==r0+sub,G[g][0],0.0),axis=1,keepdims=True)
                rs=lax.rsqrt(d)
                G[g][0]=jnp.where(lane>=r0+sub,G[g][0]*rs,0.0)
                for h in range(1,len(G[g])): G[g][h]=G[g][h]*rs
                row=jnp.concatenate(G[g],axis=1)
                a_ref[m,r0:r0+8,:]=row
                full.append(row)
            if (k+1)*b<K:
                R=jnp.concatenate(full,axis=0)
                left=R[:,:K].T[(k+1)*b:,:]
                a_ref[m,(k+1)*b:,:]=a_ref[m,(k+1)*b:,:]-jnp.dot(left,R,precision=lax.Precision.HIGHEST,preferred_element_type=jnp.float32)


def factor_kernel(grams_ref, c_ref, leaf_ref, out_ref, a_ref, f_ref):
    count = grams_ref.shape[0]
    a_ref[0:count] = grams_ref[...]
    a_ref[count] = c_ref[...]
    factor_many(a_ref, list(range(count + 1)), 16)
    core = lax.axis_index("probe")
    half = pl.ds(pl.multiple_of(core * K, K), K)
    for m in range(count):
        leaf_ref[m] = a_ref[m, :, half].T
    f_ref[...] = a_ref[count].T
    out_ref[...] = f_ref[pl.ds(lax.axis_index("rows") * 2 + core, 1), :]


def factor(grams, root_gram):
    count = grams.shape[0]
    whole = pl.BlockSpec(memory_space=pltpu.VMEM)
    return pl.pallas_call(
        factor_kernel,
        out_shape=(
            jax.ShapeDtypeStruct((count, K, K), jnp.float32),
            jax.ShapeDtypeStruct((1, K), jnp.float32),
        ),
        in_specs=[whole, whole],
        out_specs=(whole, whole),
        scratch_shapes=[
            pltpu.VMEM((count + 1, K, 2 * K), jnp.float32),
            pltpu.VMEM((2 * K, K), jnp.float32),
        ],
        name="factor",
    )(grams, root_gram)


def local(probe_matrix, near_blocks, block_cols):
    sample, grams, root_gram = gather(block_cols, probe_matrix, near_blocks)
    leaf_out, root_out = factor(grams, root_gram)
    return (sample, leaf_out, root_out)


def solution(mesh):
    placed = (P("probe", "rows"), P("rows", "probe", None, None), P("rows", "probe"))
    return jax.shard_map(
        local,
        mesh=mesh,
        in_specs=placed,
        out_specs=(P("probe", "rows"), P("rows", "probe", None), P(("rows", "probe"), None)),
        check_vma=False,
    )
```

time: 359 us -> 84.2 us (0.23)
  waiting for transfers between devices: 281 us -> 0 us
  Pallas kernels: 22 us -> 75 us
  matrix products: 14.3 us -> 0 us
  between operations: 13.9 us -> 0.66 us
  local copies, waits for them, and re-layouts: 14 us -> 7.51 us
  starting transfers between devices: 6.24 us -> 0 us
    psum x1 -> x0, waiting for transfers between devices: 208 us -> none  [local(): root_gram = lax.psum(jnp.sum(leaf_grams, axis=0), 'rows')]
    pallas_call x1 -> x2, Pallas kernels: 22 us -> 75 us  [the longest x1 53.2 us: gather(): pl.pallas_call(functools.partial(gather_kernel, depth), out_shape=(jax.Sh...]
    all_gather x2 -> x0, waiting for transfers between devices: 48.7 us -> none  [the longest x1 29.6 us: local(): rows_piece = lax.all_gather(extended, 'probe', axis=0, tiled=True)]
    reduce_scatter x1 -> x0, waiting for transfers between devices: 16.2 us -> none  [local(): lax.psum_scatter(partial_sample, 'probe', scatter_dimension=1, tiled=True)]
    dot_general x2 -> x0, matrix products: 14.3 us -> none  [the longest x1 9.51 us: local(): jnp.einsum('cnij,pcnj->cpi', near_blocks, picked_tiles, preferred_element...]
    ppermute x2 -> x0, waiting for transfers between devices: 8.23 us -> none  [the longest x1 7.33 us: with_halo(): lax.ppermute(lax.slice_in_dim(block, 0, width, axis=dim), axis, backward)]
    ppermute x2 -> x0, starting transfers between devices: 5.9 us -> none  [the longest x1 4.61 us: with_halo(): lax.ppermute(lax.slice_in_dim(block, block.shape[dim] - width, None, axis...]
    gather x1 -> x0, local copies, waits for them, and re-layouts: 5.52 us -> none  [local(): picked_tiles = jnp.take(tile_rows, local_cols, axis=1)]
  transfers between devices with their start and end apart: 6 -> 0, of which waited for: 6 -> 0; matrix products, arithmetic and copies ran while one was open for 0% -> 0% of each run, Pallas kernels for 0% -> 0%
where the time goes in v2:
time: 84.2 us; the launch traced here: 83.1 us
  Pallas kernels  75 us (89%)
  local copies, waits for them, and re-layouts  7.51 us (9%)
    pallas_call x1, Pallas kernels, gather(): pl.pallas_call(functools.partial(gather_kernel, depth), out_shape=(jax.Sh...  53.2 us
    pallas_call x1, Pallas kernels, factor(): pl.pallas_call(factor_kernel, out_shape=(jax.ShapeDtypeStruct((count, K,...  21.8 us
    unnamed x11, local copies, waits for them, and re-layouts  7.51 us

profile of v2, /device:TPU:1, one launch (start us, length us, event | category | flops | bytes accessed | tf_op | source)
XLA Modules:
  0.0 83.1 jit_solution(10047200318990652350)
XLA Ops:
  0.6 0.0 copy-start
  0.6 3.4 %copy-done = bf16[8,8,256,256]{3,2,1,0:T(8,128)(2,1)S(1)} copy-done((bf16[8,8,256,256]{3,2,1,0:T(8,128)(2,1)S(1)}, bf16[8,8,256,256]{3,2,1,0:T(8,128)(2,1)}, u32[]{:S(2)}) %copy-start) | copy-done | bytes 8388632
  4.0 0.0 copy-start.2
  4.0 1.0 %copy-done.2 = bf16[128,2048]{1,0:T(8,128)(2,1)S(1)} copy-done((bf16[128,2048]{1,0:T(8,128)(2,1)S(1)}, bf16[128,2048]{1,0:T(8,128)(2,1)}, u32[]{:S(2)}) %copy-start.2) | copy-done | bytes 524312
  5.1 0.0 copy-start.4
  5.1 0.7 copy-done.4
  5.7 53.2 %gather.1 = (bf16[128,2048]{1,0:T(8,128)(2,1)S(1)}, f32[8,128,256]{2,1,0:T(8,128)S(1)}, f32[128,256]{1,0:T(8,128)S(1)}) custom-call(s32[8,8]{1,0:T(8,128)S(1)} %copy-done.4, bf16[128,2048]{1,0:T(8,128)(2,1)S(1)} %copy-done.2, bf16[8,8,256,256]{3,2,1,0:T(8,128)(2,1)S(1)} %copy-done), custom_call_target="tpu_custom_call" | custom-call | tf_op jit(solution)/shard_map/gather/pallas_call | solution.py:190
  59.0 0.0 copy-start.1
  59.0 1.0 %copy-done.1 = f32[8,128,256]{2,1,0:T(8,128)} copy-done((f32[8,128,256]{2,1,0:T(8,128)}, f32[8,128,256]{2,1,0:T(8,128)S(1)}, u32[]{:S(2)}) %copy-start.1) | copy-done | bytes 1048600
  59.9 0.0 copy-start.3
  59.9 0.7 copy-done.3
  60.6 21.8 %factor.1 = (f32[8,128,128]{2,1,0:T(8,128)}, f32[1,128]{1,0:T(1,128)}) custom-call(f32[8,128,256]{2,1,0:T(8,128)} %copy-done.1, f32[128,256]{1,0:T(8,128)} %copy-done.3), custom_call_target="tpu_custom_call" | custom-call | tf_op jit(solution)/shard_map/factor/pallas_call | solution.py:287
  82.4 0.8 copy.7
Async XLA Ops:
  0.6 3.4 %copy-start = (bf16[8,8,256,256]{3,2,1,0:T(8,128)(2,1)S(1)}, bf16[8,8,256,256]{3,2,1,0:T(8,128)(2,1)}, u32[]{:S(2)}) copy-start(bf16[8,8,256,256]{3,2,1,0:T(8,128)(2,1)} %blocks_ref.1) | copy-start | bytes 25165828
  4.0 1.0 %copy-start.2 = (bf16[128,2048]{1,0:T(8,128)(2,1)S(1)}, bf16[128,2048]{1,0:T(8,128)(2,1)}, u32[]{:S(2)}) copy-start(bf16[128,2048]{1,0:T(8,128)(2,1)} %probe_ref.1) | copy-start | bytes 1572868
  5.1 0.7 copy-start.4
  59.0 1.0 %copy-start.1 = (f32[8,128,256]{2,1,0:T(8,128)}, f32[8,128,256]{2,1,0:T(8,128)S(1)}, u32[]{:S(2)}) copy-start(f32[8,128,256]{2,1,0:T(8,128)S(1)} %get-tuple-element.9.grams_ref) | copy-start | bytes 3145732
  59.9 0.7 copy-start.3

commit v3 on v2

--- a/solution.py
+++ b/solution.py
@@ -10,6 +10,7 @@
 K = 128
 LEAF = 256
 PLANE = 16
+PANEL = 16
 HIGH = lax.Precision.HIGHEST
 ORDER = (3, 4, 2, 5, 1, 6, 0, 7)
 
@@ -24,7 +25,7 @@
     depth, cols_ref, probe_ref, blocks_ref,
     sample_ref, grams_ref, root_ref,
     own, landing, window, blocks, mine, theirs, total, rs_buf, z_buf,
-    block_sem, own_sem, share_send, share_recv, halo_send, halo_recv, pass_send, pass_recv,
+    meet, block_sem, own_sem, share_send, share_recv, halo_send, halo_recv, pass_send, pass_recv,
     part_send, part_recv, rs_send, rs_recv, z_send, z_recv, ag_send, ag_recv,
 ):
     row, core = lax.axis_index("rows"), lax.axis_index("probe")
@@ -33,34 +34,32 @@
     after, before = (lax.rem(row + 1, rows), core), (lax.rem(row + rows - 1, rows), core)
     layer, spot = row // PLANE, lax.rem(row, PLANE)
 
+    side, front = lax.rem(spot, 4), spot // 4
+
     def in_plane(step):
         return (layer * PLANE + lax.rem(spot + step, PLANE), core)
 
     def in_column(step):
         return (lax.rem(layer + step, depth) * PLANE + spot, core)
 
+    along_x = [(layer * PLANE + front * 4 + lax.rem(side + d, 4), core) for d in (1, 3)]
+    along_y = [in_plane(4), in_plane(12)]
+    along_z = [in_column(1), in_column(depth - 1)]
+
+    def greet(semaphore, targets):
+        for target in targets:
+            pl.semaphore_signal(semaphore, inc=1, device_id=target, device_id_type=pl.DeviceIdType.MESH)
+
+    own_copies = {}
+    for c in (7, 0, 6, 1, 5, 2, 4, 3):
+        own_copies[c] = pltpu.make_async_copy(
+            probe_ref.at[:, c * LEAF:(c + 1) * LEAF], own.at[core, c], own_sem.at[c]
+        )
+        own_copies[c].start()
     barrier = pltpu.get_barrier_semaphore()
-    for target in (after, before, sibling):
-        pl.semaphore_signal(barrier, inc=1, device_id=target, device_id_type=pl.DeviceIdType.MESH)
-
-    def greet_plane(step, carry):
-        pl.semaphore_signal(barrier, inc=1, device_id=in_plane(step), device_id_type=pl.DeviceIdType.MESH)
-        return carry
-
-    def greet_column(step, carry):
-        pl.semaphore_signal(barrier, inc=1, device_id=in_column(step), device_id_type=pl.DeviceIdType.MESH)
-        return carry
-
-    lax.fori_loop(1, PLANE, greet_plane, 0)
-    lax.fori_loop(1, depth, greet_column, 0)
-
-    own_copy = pltpu.make_async_copy(probe_ref, own.at[core], own_sem)
-    own_copy.start()
-    block_copies = {}
-    for c in ORDER:
-        block_copies[c] = pltpu.make_async_copy(blocks_ref.at[c], blocks.at[c], block_sem.at[c])
-        block_copies[c].start()
-    pl.semaphore_wait(barrier, 3 + PLANE - 1 + depth - 1)
+    entered = [after, before, sibling] + along_x + along_y + along_z
+    greet(barrier, entered)
+    pl.semaphore_wait(barrier, len(entered))
 
     def remote(src, dst, send, recv, target):
         return pltpu.make_async_remote_copy(
@@ -68,22 +67,40 @@
             device_id=target, device_id_type=pl.DeviceIdType.MESH,
         )
 
+    rounds = [(meet.at[0], along_x, meet.at[1], along_z), (meet.at[2], along_y, meet.at[3], along_z),
+              (meet.at[4], along_y, meet.at[5], along_z)]
+
+    def announce(n):
+        greet(rounds[n][0], rounds[n][1])
+        greet(rounds[n][2], rounds[n][3])
+
+    def learn(n):
+        pl.semaphore_wait(rounds[n][0], 2)
+        pl.semaphore_wait(rounds[n][2], 2)
+
     halo = {}
+    waited = set()
     for t in range(8):
-        for side, c, target in ((0, 7 - t, after), (1, t, before)):
-            halo[side, t] = remote(
-                probe_ref.at[:, c * LEAF:(c + 1) * LEAF], landing.at[side, c, core],
-                halo_send.at[side, c], halo_recv.at[side, c], target,
+        for side_of, c, target in ((0, 7 - t, after), (1, t, before)):
+            if c not in waited:
+                own_copies[c].wait()
+                waited.add(c)
+            halo[side_of, t] = remote(
+                own.at[core, c], landing.at[side_of, c, core],
+                halo_send.at[side_of, c], halo_recv.at[side_of, c], target,
             )
-            halo[side, t].start()
-    share = remote(probe_ref, own.at[core], share_send, share_recv, sibling)
+            halo[side_of, t].start()
+    share = remote(own.at[core], own.at[core], share_send, share_recv, sibling)
     share.start()
-
-    own_copy.wait()
+    announce(0)
+    block_copies = {}
+    for c in ORDER:
+        block_copies[c] = pltpu.make_async_copy(blocks_ref.at[c], blocks.at[c], block_sem.at[c])
+        block_copies[c].start()
     share.wait_recv()
     for c in range(8):
         for half in range(2):
-            window[8 + c, half * K:(half + 1) * K, :] = own[half, :, c * LEAF:(c + 1) * LEAF]
+            window[8 + c, half * K:(half + 1) * K, :] = own[half, c]
 
     passed = {}
     parts = {}
@@ -123,6 +140,10 @@
             )
             passed[side, t].start()
         absorb(t)
+        if 1 <= t <= 3:
+            learn(t - 1)
+            if t < 3:
+                announce(t)
         if t >= 4:
             for c in (7 - t, t):
                 multiply(c)
@@ -196,12 +217,12 @@
         ),
         in_specs=[
             pl.BlockSpec(memory_space=pltpu.SMEM),
-            pl.BlockSpec(memory_space=pl.ANY),
-            pl.BlockSpec(memory_space=pl.ANY),
+            pl.BlockSpec(memory_space=pltpu.HBM),
+            pl.BlockSpec(memory_space=pltpu.HBM),
         ],
         out_specs=(whole, whole, whole),
         scratch_shapes=[
-            pltpu.VMEM((2, K, 8 * LEAF), bf16),
+            pltpu.VMEM((2, 8, K, LEAF), bf16),
             pltpu.VMEM((2, 8, 2, K, LEAF), bf16),
             pltpu.VMEM((24, LEAF, LEAF), bf16),
             pltpu.VMEM((8, 8, LEAF, LEAF), bf16),
@@ -210,80 +231,93 @@
             pltpu.VMEM((K, LEAF), f32),
             pltpu.VMEM((PLANE, 8, LEAF), f32),
             pltpu.VMEM((depth, 8, LEAF), f32),
-            dma((8,)), dma, dma, dma, dma((2, 8)), dma((2, 8)), dma((2, 8)), dma((2, 8)),
+            pltpu.SemaphoreType.REGULAR((6,)), dma((8,)), dma((8,)), dma, dma, dma((2, 8)), dma((2, 8)), dma((2, 8)), dma((2, 8)),
             dma((8,)), dma((8,)), dma((PLANE,)), dma((PLANE,)),
             dma((depth,)), dma((depth,)), dma((PLANE,)), dma((PLANE,)),
         ],
         compiler_params=pltpu.CompilerParams(
-            collective_id=0, has_side_effects=True, vmem_limit_bytes=40 * 2**20
+            collective_id=0, has_side_effects=True, vmem_limit_bytes=56 * 2**20
         ),
         name="gather",
     )(block_cols, probe_matrix, near_blocks)
 
 
-def eliminate_panel(groups, first, ncols):
-    ng=len(groups)
-    iota=lax.broadcasted_iota(jnp.int32,(8,K),0)
-    W=groups[0].shape[1]
-    nh=W//K
-    G=[[g[:,h*K:(h+1)*K] for h in range(nh)] for g in groups]
-    for j in range(8*ng):
-        c=first+j; gj,sj=divmod(j,8)
-        bc=jnp.broadcast_to(G[gj][0][:,c:c+1],(8,K))
-        inv=1.0/bc[sj:sj+1,:]
-        rows=[G[gj][h][sj:sj+1,:]*inv for h in range(nh)]
-        for g in range(gj,ng):
-            if g==gj:
-                if sj==7: continue
-                m=jnp.where(iota>sj,bc,0.0)
+SUB = 8
+
+
+def eliminate_block(rows, c0, bs):
+    e={}
+    for j in range(bs):
+        for i in range(j,bs):
+            e[j,i]=jnp.broadcast_to(rows[j][0][:,c0+i:c0+i+1],(SUB,K))
+    for j in range(bs):
+        rs=lax.rsqrt(e[j,j])
+        f={i:e[j,i]*rs for i in range(j+1,bs)}
+        rows[j]=[h*rs for h in rows[j]]
+        for i in range(j+1,bs):
+            for i2 in range(i,bs):
+                e[i,i2]=e[i,i2]-f[i]*f[i2]
+            rows[i]=[h-f[i]*p for h,p in zip(rows[i],rows[j])]
+    for i in range(bs,len(rows)):
+        for j in range(bs):
+            f=jnp.broadcast_to(rows[j][0][:,c0+i:c0+i+1],(SUB,K))
+            rows[i]=[h-f*p for h,p in zip(rows[i],rows[j])]
+    return rows
+def factor_groups(a_refs, t_refs, b, bs):
+    lane=lax.broadcasted_iota(jnp.int32,(b,K),1)
+    sub=lax.broadcasted_iota(jnp.int32,(b,K),0)
+    for k in range(K//b):
+        r0=k*b
+        panels=[]
+        for (a_ref,m),(t0,t1) in zip(a_refs,t_refs):
+            rows=[]
+            if m==1:
+                for r in range(b):
+                    rows.append([jnp.broadcast_to(a_ref[0,r0+r:r0+r+1,h*K:(h+1)*K],(SUB,K)) for h in range(2)])
             else:
-                m=jnp.broadcast_to(G[g][0][:,c:c+1],(8,K))
-            for h in range(nh):
-                G[g][h]=G[g][h]-m*rows[h]
-    return G
-def factor_many(a_ref, ms, b, W=2*K):
-    ng=b//8
-    lane=lax.broadcasted_iota(jnp.int32,(8,K),1)
-    sub=lax.broadcasted_iota(jnp.int32,(8,K),0)
-    for k in range(K//b):
-        outs=[]
-        for m in ms:
-            P=[a_ref[m,k*b+8*g:k*b+8*g+8,:] for g in range(ng)]
-            outs.append(P)
-        res=[eliminate_panel(P,k*b,b) for P in outs]
-        for m,G in zip(ms,res):
-            full=[]
-            for g in range(ng):
-                r0=k*b+8*g
-                d=jnp.sum(jnp.where(lane==r0+sub,G[g][0],0.0),axis=1,keepdims=True)
-                rs=lax.rsqrt(d)
-                G[g][0]=jnp.where(lane>=r0+sub,G[g][0]*rs,0.0)
-                for h in range(1,len(G[g])): G[g][h]=G[g][h]*rs
-                row=jnp.concatenate(G[g],axis=1)
-                a_ref[m,r0:r0+8,:]=row
-                full.append(row)
-            if (k+1)*b<K:
-                R=jnp.concatenate(full,axis=0)
-                left=R[:,:K].T[(k+1)*b:,:]
-                a_ref[m,(k+1)*b:,:]=a_ref[m,(k+1)*b:,:]-jnp.dot(left,R,precision=lax.Precision.HIGHEST,preferred_element_type=jnp.float32)
-
-
-def factor_kernel(grams_ref, c_ref, leaf_ref, out_ref, a_ref, f_ref):
+                for s in range(m):
+                    t0[pl.ds(s,b,stride=SUB),:]=a_ref[s,r0:r0+b,0:K]
+                    t1[pl.ds(s,b,stride=SUB),:]=a_ref[s,r0:r0+b,K:2*K]
+                for r in range(b):
+                    rows.append([t[SUB*r:SUB*r+SUB,:] for t in (t0,t1)])
+            panels.append(rows)
+        for c in range(0,b,bs):
+            for g in range(len(panels)):
+                rest=eliminate_block(panels[g][c:],r0+c,bs)
+                panels[g]=panels[g][:c]+rest
+        for (a_ref,m),(t0,t1),rows in zip(a_refs,t_refs,panels):
+            for r in range(b):
+                t0[SUB*r:SUB*r+SUB,:]=rows[r][0]
+                t1[SUB*r:SUB*r+SUB,:]=rows[r][1]
+            for s in range(m):
+                low=t0[pl.ds(s,b,stride=SUB),:]
+                high=t1[pl.ds(s,b,stride=SUB),:]
+                low=jnp.where(lane>=r0+sub,low,0.0)
+                a_ref[s,r0:r0+b,0:K]=low
+                a_ref[s,r0:r0+b,K:2*K]=high
+                if r0+b<K:
+                    left=low.T[r0+b:,:]
+                    right=jnp.concatenate([low,high],axis=1)
+                    a_ref[s,r0+b:,:]=a_ref[s,r0+b:,:]-jnp.dot(left,right,precision=lax.Precision.HIGHEST,preferred_element_type=jnp.float32)
+
+
+def factor_kernel(grams_ref, c_ref, leaf_ref, out_ref, a_ref, r_ref, f_ref, t0, t1, t2, t3):
     count = grams_ref.shape[0]
-    a_ref[0:count] = grams_ref[...]
-    a_ref[count] = c_ref[...]
-    factor_many(a_ref, list(range(count + 1)), 16)
+    a_ref[...] = grams_ref[...]
+    r_ref[0] = c_ref[...]
+    factor_groups([(a_ref, count), (r_ref, 1)], [(t0, t1), (t2, t3)], PANEL, 8)
     core = lax.axis_index("probe")
     half = pl.ds(pl.multiple_of(core * K, K), K)
     for m in range(count):
         leaf_ref[m] = a_ref[m, :, half].T
-    f_ref[...] = a_ref[count].T
+    f_ref[...] = r_ref[0].T
     out_ref[...] = f_ref[pl.ds(lax.axis_index("rows") * 2 + core, 1), :]
 
 
 def factor(grams, root_gram):
     count = grams.shape[0]
     whole = pl.BlockSpec(memory_space=pltpu.VMEM)
+    rows = pltpu.VMEM((PANEL * SUB, K), jnp.float32)
     return pl.pallas_call(
         factor_kernel,
         out_shape=(
@@ -293,8 +327,10 @@
         in_specs=[whole, whole],
         out_specs=(whole, whole),
         scratch_shapes=[
-            pltpu.VMEM((count + 1, K, 2 * K), jnp.float32),
+            pltpu.VMEM((count, K, 2 * K), jnp.float32),
+            pltpu.VMEM((1, K, 2 * K), jnp.float32),
             pltpu.VMEM((2 * K, K), jnp.float32),
+            rows, rows, rows, rows,
         ],
         name="factor",
     )(grams, root_gram)

time: 84.2 us -> 69 us (0.82)
  Pallas kernels: 75 us -> 65.2 us
  local copies, waits for them, and re-layouts: 7.51 us -> 1.88 us
    pallas_call x1, Pallas kernels: 21.8 us -> 11.8 us  [factor(): pl.pallas_call(factor_kernel, out_shape=(jax.ShapeDtypeStruct((count, K,...]
    unnamed x11 -> x1, local copies, waits for them, and re-layouts: 7.51 us -> 1.88 us
where the time goes in v3:
time: 69 us; the launch traced here: 67.7 us
  Pallas kernels  65.2 us (94%)
  local copies, waits for them, and re-layouts  1.88 us (3%)
    pallas_call x1, Pallas kernels, gather(): pl.pallas_call(functools.partial(gather_kernel, depth), out_shape=(jax.Sh...  53.4 us
    pallas_call x1, Pallas kernels, factor(): pl.pallas_call(factor_kernel, out_shape=(jax.ShapeDtypeStruct((count, K,...  11.8 us
    unnamed x1, local copies, waits for them, and re-layouts  1.88 us

profile of v3, /device:TPU:1, one launch (start us, length us, event | category | flops | bytes accessed | tf_op | source)
XLA Modules:
  0.0 67.7 jit_solution(8934156806512337422)
XLA Ops:
  0.6 53.4 %gather.1 = (bf16[128,2048]{1,0:T(8,128)(2,1)}, f32[8,128,256]{2,1,0:T(8,128)}, f32[128,256]{1,0:T(8,128)}) custom-call(s32[8,8]{1,0:T(8,128)} %cols_ref.1, bf16[128,2048]{1,0:T(8,128)(2,1)} %probe_ref.1, bf16[8,8,256,256]{3,2,1,0:T(8,128)(2,1)} %blocks_ref.1), custom_call_target="tpu_custom_call" | custom-call | tf_op jit(solution)/shard_map/gather/pallas_call | solution.py:211
  54.0 11.8 %factor.1 = (f32[8,128,128]{2,1,0:T(8,128)}, f32[1,128]{1,0:T(1,128)}) custom-call(f32[8,128,256]{2,1,0:T(8,128)} %get-tuple-element.9.grams_ref, f32[128,256]{1,0:T(8,128)} %get-tuple-element.10.c_ref), custom_call_target="tpu_custom_call" | custom-call | tf_op jit(solution)/shard_map/factor/pallas_call | solution.py:321
  65.8 1.9 %copy.7 = bf16[128,2048]{1,0:T(8,128)(2,1)} copy(bf16[128,2048]{1,0:T(8,128)(2,1)} %get-tuple-element.16) | data formatting | bytes 1048576

commit v4 on v0

v4 whole, which is shorter than its diff:
```python
import functools

import jax
import jax.numpy as jnp
from jax import lax
from jax.experimental import pallas as pl
from jax.experimental.pallas import tpu as pltpu
from jax.sharding import PartitionSpec as P

K = 128
LEAF = 256
PLANE = 16
PANEL = 16
BLOCK = 8
SUB = 8
HIGH = lax.Precision.HIGHEST
MESH = pl.DeviceIdType.MESH


def cross(a, b, precision=None):
    return lax.dot_general(
        a, b, (((1,), (1,)), ((), ())), precision=precision, preferred_element_type=jnp.float32
    )


def eliminate_block(rows, c0):
    e = {}
    for j in range(BLOCK):
        for i in range(j, BLOCK):
            e[j, i] = jnp.broadcast_to(rows[j][0][:, c0 + i:c0 + i + 1], (SUB, K))
    for j in range(BLOCK):
        rs = lax.rsqrt(e[j, j])
        f = {i: e[j, i] * rs for i in range(j + 1, BLOCK)}
        rows[j] = [h * rs for h in rows[j]]
        for i in range(j + 1, BLOCK):
            for i2 in range(i, BLOCK):
                e[i, i2] = e[i, i2] - f[i] * f[i2]
            rows[i] = [h - f[i] * p for h, p in zip(rows[i], rows[j])]
    for i in range(BLOCK, len(rows)):
        for j in range(BLOCK):
            f = jnp.broadcast_to(rows[j][0][:, c0 + i:c0 + i + 1], (SUB, K))
            rows[i] = [h - f * p for h, p in zip(rows[i], rows[j])]
    return rows


def factor_panel(a_ref, count, t0, t1, k):
    r0 = k * PANEL
    lane = lax.broadcasted_iota(jnp.int32, (PANEL, K), 1)
    sub = lax.broadcasted_iota(jnp.int32, (PANEL, K), 0)
    if count == 1:
        rows = [
            [jnp.broadcast_to(a_ref[0, r0 + r:r0 + r + 1, h * K:(h + 1) * K], (SUB, K)) for h in range(2)]
            for r in range(PANEL)
        ]
    else:
        for s in range(count):
            t0[pl.ds(s, PANEL, stride=SUB), :] = a_ref[s, r0:r0 + PANEL, 0:K]
            t1[pl.ds(s, PANEL, stride=SUB), :] = a_ref[s, r0:r0 + PANEL, K:2 * K]
        rows = [[t[SUB * r:SUB * r + SUB, :] for t in (t0, t1)] for r in range(PANEL)]
    for c in range(0, PANEL, BLOCK):
        rows = rows[:c] + eliminate_block(rows[c:], r0 + c)
    for r in range(PANEL):
        t0[SUB * r:SUB * r + SUB, :] = rows[r][0]
        t1[SUB * r:SUB * r + SUB, :] = rows[r][1]
    for s in range(count):
        low = jnp.where(lane >= r0 + sub, t0[pl.ds(s, PANEL, stride=SUB), :], 0.0)
        high = t1[pl.ds(s, PANEL, stride=SUB), :]
        a_ref[s, r0:r0 + PANEL, 0:K] = low
        a_ref[s, r0:r0 + PANEL, K:2 * K] = high
        if r0 + PANEL < K:
            left = low.T[r0 + PANEL:, :]
            right = jnp.concatenate([low, high], axis=1)
            a_ref[s, r0 + PANEL:, :] = a_ref[s, r0 + PANEL:, :] - jnp.dot(
                left, right, precision=HIGH, preferred_element_type=jnp.float32
            )


def gather_kernel(
    depth, cols_ref, probe_ref, blocks_ref,
    sample_ref, leaf_ref, root_ref,
    own, landing, window, blocks, given, kept, theirs, stage, sent_stage, total, rs_buf, z_buf,
    leaf_a, t0, t1, leaf_buf, sent_leaf,
    meet, block_sem, own_sem, share_send, share_recv, halo_send, halo_recv, pass_send, pass_recv,
    part_send, part_recv, tile_send, tile_recv, out_sem, leaf_send, leaf_recv, leaf_sem,
    rs_send, rs_recv, z_send, z_recv, ag_send, ag_recv,
):
    row, core = lax.axis_index("rows"), lax.axis_index("probe")
    rows = PLANE * depth
    sibling = (row, 1 - core)
    after, before = (lax.rem(row + 1, rows), core), (lax.rem(row + rows - 1, rows), core)
    layer, spot = row // PLANE, lax.rem(row, PLANE)
    side, front = lax.rem(spot, 4), spot // 4

    def in_plane(step):
        return (layer * PLANE + lax.rem(spot + step, PLANE), core)

    def in_column(step):
        return (lax.rem(layer + step, depth) * PLANE + spot, lax.rem(core + step // depth, 2))

    along_x = [(layer * PLANE + front * 4 + lax.rem(side + d, 4), core) for d in (1, 3)]
    along_y = [in_plane(4), in_plane(12)]
    along_z = [in_column(1), in_column(depth - 1)]

    def greet(semaphore, targets):
        for target in targets:
            pl.semaphore_signal(semaphore, inc=1, device_id=target, device_id_type=MESH)

    def remote(src, dst, send, recv, target):
        return pltpu.make_async_remote_copy(
            src_ref=src, dst_ref=dst, send_sem=send, recv_sem=recv,
            device_id=target, device_id_type=MESH,
        )

    own_copies = {}
    for c in (7, 0, 6, 1, 5, 2, 4, 3):
        own_copies[c] = pltpu.make_async_copy(
            probe_ref.at[:, c * LEAF:(c + 1) * LEAF], own.at[core, c], own_sem.at[c]
        )
        own_copies[c].start()
    barrier = pltpu.get_barrier_semaphore()
    entered = [after, before, sibling] + along_x + along_y + along_z
    greet(barrier, entered)
    pl.semaphore_wait(barrier, len(entered))

    rounds = [
        ((meet.at[0], along_x), (meet.at[1], along_z)),
        ((meet.at[2], along_y), (meet.at[3], along_z)),
        ((meet.at[4], along_y), (meet.at[5], along_z)),
        ((meet.at[6], [sibling]),),
    ]

    def announce(n):
        for semaphore, targets in rounds[n]:
            greet(semaphore, targets)

    def learn(n):
        for semaphore, targets in rounds[n]:
            pl.semaphore_wait(semaphore, len(targets))

    halo = {}
    waited = set()
    for t in range(8):
        for which, c, target in ((0, 7 - t, after), (1, t, before)):
            if c not in waited:
                own_copies[c].wait()
                waited.add(c)
            halo[which, t] = remote(
                own.at[core, c], landing.at[which, c, core],
                halo_send.at[which, c], halo_recv.at[which, c], target,
            )
            halo[which, t].start()
    share = remote(own.at[core], own.at[core], share_send, share_recv, sibling)
    share.start()
    announce(0)

    def mine(n):
        return (1 - core) * (3 - n) + core * (4 + n)

    def block_copy(c):
        return pltpu.make_async_copy(blocks_ref.at[c], blocks.at[c], block_sem.at[c])

    for c in (3, 4, 2, 5, 1, 6, 0, 7):
        block_copy(c).start()
    share.wait_recv()
    for c in range(8):
        for half in range(2):
            window[8 + c, half * K:(half + 1) * K, :] = own[half, c]

    passed, parts, tiles = {}, {}, {}

    def absorb(t):
        for which, c in ((0, 7 - t), (1, t)):
            passed[which, t].wait_recv()
            for half in range(2):
                window[16 * which + c, half * K:(half + 1) * K, :] = landing[which, c, half]

    def product(c):
        acc = jnp.zeros((LEAF, LEAF), jnp.float32)
        for b in range(8):
            at = jnp.clip(cols_ref[c, b] - (row * 8 - 8), 0, 23)
            acc = acc + cross(window[at], blocks[c, b])
        return acc

    def multiply(n):
        block_copy(3 - n).wait()
        block_copy(4 + n).wait()
        given[n] = product(7 - mine(n))
        parts[n] = remote(given.at[n], theirs.at[n], part_send.at[n], part_recv.at[n], sibling)
        parts[n].start()
        kept[n] = product(mine(n))

    def sample_out(n, c):
        at = pl.multiple_of(c * LEAF, LEAF)
        return pltpu.make_async_copy(stage.at[c], sample_ref.at[:, pl.ds(at, LEAF)], out_sem.at[n])

    def finish(n):
        c = mine(n)
        parts[n].wait_recv()
        full = kept[n] + theirs[n]
        kept[n] = full
        gram = cross(full[:K], full, HIGH)
        leaf_a[n] = gram
        total[...] = gram if n == 0 else total[...] + gram

    def hand_out(n):
        c = mine(n)
        stage[c] = kept[n, pl.ds(pl.multiple_of(core * K, K), K), :].astype(jnp.bfloat16)
        sent_stage[n] = kept[n, pl.ds(pl.multiple_of((1 - core) * K, K), K), :].astype(jnp.bfloat16)
        tiles[n] = remote(sent_stage.at[n], stage.at[c], tile_send.at[n], tile_recv.at[n], sibling)
        tiles[n].start()
        sample_out(n, c).start()

    for t in range(9):
        if t < 8:
            for which, c in ((0, 7 - t), (1, t)):
                halo[which, t].wait_recv()
                passed[which, t] = remote(
                    landing.at[which, c, core], landing.at[which, c, core],
                    pass_send.at[which, c], pass_recv.at[which, c], sibling,
                )
                passed[which, t].start()
        if t >= 1:
            absorb(t - 1)
        if 1 <= t <= 4:
            learn(t - 1)
            if t < 4:
                announce(t)
        if t >= 5:
            multiply(t - 5)
        if t >= 6:
            finish(t - 6)
            if t < 8:
                hand_out(t - 6)
    finish(3)

    def scatter(step):
        at = pl.multiple_of(lax.rem(spot + step, PLANE) * 8, 8)
        return remote(total.at[pl.ds(at, 8), :], rs_buf.at[step], rs_send.at[step], rs_recv.at[step], in_plane(step))

    def column(step):
        return remote(z_buf.at[0], z_buf.at[step], z_send.at[step], z_recv.at[step], in_column(step))

    here = pl.ds(pl.multiple_of(spot * 8, 8), 8)

    def publish(step):
        return remote(root_ref.at[here, :], root_ref.at[here, :], ag_send.at[step], ag_recv.at[step], in_plane(step))

    def published(step):
        place = pl.ds(pl.multiple_of(lax.rem(spot + PLANE - step, PLANE) * 8, 8), 8)
        return remote(root_ref.at[place, :], root_ref.at[place, :], ag_send.at[step], ag_recv.at[step], in_plane(step))

    def each(count, act):
        def body(step, carry):
            act(step)
            return carry

        lax.fori_loop(1, count, body, 0)

    each(PLANE, lambda step: scatter(step).start())
    rs_buf[0] = total[here, :]
    hand_out(2)
    hand_out(3)
    t0[...] = jnp.zeros_like(t0)
    t1[...] = jnp.zeros_like(t1)
    for k in range(0, 3):
        factor_panel(leaf_a, 4, t0, t1, k)
    each(PLANE, lambda step: scatter(step).wait())
    z_buf[0] = jnp.sum(rs_buf[...], axis=0)
    each(2 * depth, lambda step: column(step).start())
    for n in range(4):
        tiles[n].wait_recv()
        sample_out(4 + n, 7 - mine(n)).start()
    for k in range(3, 6):
        factor_panel(leaf_a, 4, t0, t1, k)
    each(2 * depth, lambda step: column(step).wait())
    root_ref[here, :] = jnp.sum(z_buf[...], axis=0)
    each(PLANE, lambda step: publish(step).start())
    for k in range(6, 8):
        factor_panel(leaf_a, 4, t0, t1, k)
    leaves = []
    for n in range(4):
        sent_leaf[n] = leaf_a[n, :, pl.ds(pl.multiple_of((1 - core) * K, K), K)].T
        leaves.append(remote(sent_leaf.at[n], leaf_buf.at[mine(n)], leaf_send.at[n], leaf_recv.at[n], sibling))
        leaves[n].start()
        leaf_buf[mine(n)] = leaf_a[n, :, pl.ds(pl.multiple_of(core * K, K), K)].T
    for n in range(4):
        leaves[n].wait_recv()
    leaf_out = pltpu.make_async_copy(leaf_buf, leaf_ref, leaf_sem)
    leaf_out.start()

    def close(step):
        publish(step).wait_send()
        published(step).wait_recv()

    each(PLANE, close)
    share.wait_send()
    for copy in list(halo.values()) + list(passed.values()) + list(parts.values()) + list(tiles.values()) + leaves:
        copy.wait_send()
    for n in range(4):
        sample_out(n, mine(n)).wait()
        sample_out(4 + n, 7 - mine(n)).wait()
    leaf_out.wait()


def gather(block_cols, probe_matrix, near_blocks):
    depth = lax.axis_size("rows") // PLANE
    bf16, f32, dma = jnp.bfloat16, jnp.float32, pltpu.SemaphoreType.DMA
    hbm = pl.BlockSpec(memory_space=pltpu.HBM)
    return pl.pallas_call(
        functools.partial(gather_kernel, depth),
        out_shape=(
            jax.ShapeDtypeStruct((K, 8 * LEAF), bf16),
            jax.ShapeDtypeStruct((8, K, K), f32),
            jax.ShapeDtypeStruct((K, LEAF), f32),
        ),
        in_specs=[pl.BlockSpec(memory_space=pltpu.SMEM), hbm, hbm],
        out_specs=(hbm, hbm, pl.BlockSpec(memory_space=pltpu.VMEM)),
        scratch_shapes=[
            pltpu.VMEM((2, 8, K, LEAF), bf16),
            pltpu.VMEM((2, 8, 2, K, LEAF), bf16),
            pltpu.VMEM((24, LEAF, LEAF), bf16),
            pltpu.VMEM((8, 8, LEAF, LEAF), bf16),
            pltpu.VMEM((4, LEAF, LEAF), f32),
            pltpu.VMEM((4, LEAF, LEAF), f32),
            pltpu.VMEM((4, LEAF, LEAF), f32),
            pltpu.VMEM((8, K, LEAF), bf16),
            pltpu.VMEM((4, K, LEAF), bf16),
            pltpu.VMEM((K, LEAF), f32),
            pltpu.VMEM((PLANE, 8, LEAF), f32),
            pltpu.VMEM((2 * depth, 8, LEAF), f32),
            pltpu.VMEM((4, K, 2 * K), f32),
            pltpu.VMEM((PANEL * SUB, K), f32),
            pltpu.VMEM((PANEL * SUB, K), f32),
            pltpu.VMEM((8, K, K), f32),
            pltpu.VMEM((4, K, K), f32),
            pltpu.SemaphoreType.REGULAR((7,)),
            dma((8,)), dma((8,)), dma, dma, dma((2, 8)), dma((2, 8)), dma((2, 8)), dma((2, 8)),
            dma((4,)), dma((4,)), dma((4,)), dma((4,)), dma((8,)), dma((4,)), dma((4,)), dma,
            dma((PLANE,)), dma((PLANE,)), dma((2 * depth,)), dma((2 * depth,)), dma((PLANE,)), dma((PLANE,)),
        ],
        compiler_params=pltpu.CompilerParams(
            collective_id=0, has_side_effects=True, vmem_limit_bytes=56 * 2**20
        ),
        name="gather",
    )(block_cols, probe_matrix, near_blocks)


def factor_kernel(c_ref, sample_in, leaf_in, sample_ref, leaf_ref, out_ref, r_ref, f_ref, t0, t1, sems):
    copies = [
        pltpu.make_async_copy(sample_in, sample_ref, sems.at[0]),
        pltpu.make_async_copy(leaf_in, leaf_ref, sems.at[1]),
    ]
    for copy in copies:
        copy.start()
    r_ref[0] = c_ref[...]
    for k in range(K // PANEL):
        factor_panel(r_ref, 1, t0, t1, k)
    f_ref[...] = r_ref[0].T
    out_ref[...] = f_ref[pl.ds(lax.axis_index("rows") * 2 + lax.axis_index("probe"), 1), :]
    for copy in copies:
        copy.wait()


def factor(root_gram, sample, leaf):
    whole, hbm = pl.BlockSpec(memory_space=pltpu.VMEM), pl.BlockSpec(memory_space=pltpu.HBM)
    rows = pltpu.VMEM((PANEL * SUB, K), jnp.float32)
    return pl.pallas_call(
        factor_kernel,
        out_shape=(
            jax.ShapeDtypeStruct(sample.shape, sample.dtype),
            jax.ShapeDtypeStruct(leaf.shape, leaf.dtype),
            jax.ShapeDtypeStruct((1, K), jnp.float32),
        ),
        in_specs=[whole, hbm, hbm],
        out_specs=(hbm, hbm, whole),
        scratch_shapes=[
            pltpu.VMEM((1, K, 2 * K), jnp.float32),
            pltpu.VMEM((2 * K, K), jnp.float32),
            rows, rows, pltpu.SemaphoreType.DMA((2,)),
        ],
        name="factor",
    )(root_gram, sample, leaf)


def local(probe_matrix, near_blocks, block_cols):
    sample, leaf, root_gram = gather(block_cols, probe_matrix, near_blocks)
    return factor(root_gram, sample, leaf)


def solution(mesh):
    placed = (P("probe", "rows"), P("rows", "probe", None, None), P("rows", "probe"))
    return jax.shard_map(
        local,
        mesh=mesh,
        in_specs=placed,
        out_specs=(P("probe", "rows"), P("rows", "probe", None), P(("rows", "probe"), None)),
        check_vma=False,
    )
```

time: 526 us -> 85.3 us (0.16); the launches traced: 517 us -> 85.1 us
  other arithmetic: 358 us -> 0 us
  Pallas kernels: 0 us -> 84.5 us
  waiting for transfers between devices: 82.5 us -> 0 us
  starting transfers between devices: 22.7 us -> 0 us
  matrix products: 22.6 us -> 0 us
  local copies, waits for them, and re-layouts: 16.9 us -> 0 us
  between operations: 14.7 us -> 0.64 us
    another operation x47 -> x0, other arithmetic: 356 us -> none  [the longest x28 193 us: finish(): lower_tri = jnp.linalg.cholesky(gram_cross[:, :, :K])]
    pallas_call x0 -> x2, Pallas kernels: none -> 84.5 us  [the longest x1 50.2 us: gather(): pl.pallas_call(functools.partial(gather_kernel, depth), out_shape=(jax.Sh...]
    all_gather x2 -> x0, waiting for transfers between devices: 44.8 us -> none  [the longest x1 25.5 us: local(): rows_piece = lax.all_gather(extended, 'probe', axis=0, tiled=True)]
    ppermute x9 -> x0, starting transfers between devices: 22.1 us -> none  [the longest x7 16.8 us: swapped(): return lax.ppermute(block, axis, route)]
    ppermute x9 -> x0, waiting for transfers between devices: 22 us -> none  [the longest x1 9.24 us: with_halo(): lax.ppermute(lax.slice_in_dim(block, block.shape[dim] - width, None, axis...]
    dot_general x10 -> x0, matrix products: 19 us -> none  [the longest x1 9.54 us: local(): jnp.einsum('cnij,pcnj->cpi', near_blocks, picked_tiles, preferred_element...]
    reduce_scatter x1 -> x0, waiting for transfers between devices: 15.7 us -> none  [local(): lax.psum_scatter(partial_sample, 'probe', scatter_dimension=1, tiled=True)]
    gather x1 -> x0, local copies, waits for them, and re-layouts: 5.52 us -> none  [local(): picked_tiles = jnp.take(tile_rows, local_cols, axis=1)]
  transfers between devices with their start and end apart: 12 -> 0, of which waited for: 9 -> 0; matrix products, arithmetic and copies ran while one was open for 35% -> 0% of each run, Pallas kernels for 0% -> 0%
where the time goes in v4:
time: 85.3 us; the launch traced here: 85.1 us
  Pallas kernels  84.5 us (99%)
    pallas_call x1, Pallas kernels, gather(): pl.pallas_call(functools.partial(gather_kernel, depth), out_shape=(jax.Sh...  50.2 us
    pallas_call x1, Pallas kernels, factor(): pl.pallas_call(factor_kernel, out_shape=(jax.ShapeDtypeStruct(sample.shap...  34.3 us

profile of v4, /device:TPU:1, one launch (start us, length us, event | category | flops | bytes accessed | tf_op | source)
XLA Modules:
  0.0 85.1 jit_solution(3955299685613182846)
XLA Ops:
  0.6 50.2 %gather.1 = (bf16[128,2048]{1,0:T(8,128)(2,1)}, f32[8,128,128]{2,1,0:T(8,128)}, f32[128,256]{1,0:T(8,128)}) custom-call(s32[8,8]{1,0:T(8,128)} %cols_ref.1, bf16[128,2048]{1,0:T(8,128)(2,1)} %probe_ref.1, bf16[8,8,256,256]{3,2,1,0:T(8,128)(2,1)} %blocks_ref.1), custom_call_target="tpu_custom_call" | custom-call | tf_op jit(solution)/shard_map/gather/pallas_call | solution.py:309
  50.8 34.3 %factor.1 = (bf16[128,2048]{1,0:T(8,128)(2,1)}, f32[8,128,128]{2,1,0:T(8,128)}, f32[1,128]{1,0:T(1,128)}) custom-call(f32[128,256]{1,0:T(8,128)} %get-tuple-element.6.c_ref, bf16[128,2048]{1,0:T(8,128)(2,1)} %get-tuple-element.7.sample_in, f32[8,128,128]{2,1,0:T(8,128)} %get-tuple-element.8.leaf_in), custom_call_target="tpu_custom_call" | custom-call | tf_op jit(solution)/shard_map/factor/pallas_call | solution.py:367

commit v5 on v4

--- a/solution.py
+++ b/solution.py
@@ -345,19 +345,28 @@
     )(block_cols, probe_matrix, near_blocks)
 
 
-def factor_kernel(c_ref, sample_in, leaf_in, sample_ref, leaf_ref, out_ref, r_ref, f_ref, t0, t1, sems):
-    copies = [
-        pltpu.make_async_copy(sample_in, sample_ref, sems.at[0]),
-        pltpu.make_async_copy(leaf_in, leaf_ref, sems.at[1]),
+def factor_kernel(c_ref, sample_in, leaf_in, sample_ref, leaf_ref, out_ref, r_ref, f_ref, t0, t1, sample_v, leaf_v, sems):
+    inward = [
+        pltpu.make_async_copy(sample_in, sample_v, sems.at[0]),
+        pltpu.make_async_copy(leaf_in, leaf_v, sems.at[1]),
     ]
-    for copy in copies:
+    outward = [
+        pltpu.make_async_copy(sample_v, sample_ref, sems.at[2]),
+        pltpu.make_async_copy(leaf_v, leaf_ref, sems.at[3]),
+    ]
+    for copy in inward:
         copy.start()
     r_ref[0] = c_ref[...]
     for k in range(K // PANEL):
         factor_panel(r_ref, 1, t0, t1, k)
+        if k == 3:
+            for copy in inward:
+                copy.wait()
+            for copy in outward:
+                copy.start()
     f_ref[...] = r_ref[0].T
     out_ref[...] = f_ref[pl.ds(lax.axis_index("rows") * 2 + lax.axis_index("probe"), 1), :]
-    for copy in copies:
+    for copy in outward:
         copy.wait()
 
 
@@ -376,7 +385,10 @@
         scratch_shapes=[
             pltpu.VMEM((1, K, 2 * K), jnp.float32),
             pltpu.VMEM((2 * K, K), jnp.float32),
-            rows, rows, pltpu.SemaphoreType.DMA((2,)),
+            rows, rows,
+            pltpu.VMEM(sample.shape, sample.dtype),
+            pltpu.VMEM(leaf.shape, leaf.dtype),
+            pltpu.SemaphoreType.DMA((4,)),
         ],
         name="factor",
     )(root_gram, sample, leaf)

time: 85.3 us -> 57.8 us (0.68)
  Pallas kernels: 84.5 us -> 56.9 us
    pallas_call x1, Pallas kernels: 34.3 us -> 6.75 us  [factor(): pl.pallas_call(factor_kernel, out_shape=(jax.ShapeDtypeStruct(sample.shap...]
where the time goes in v5:
time: 57.8 us; the launch traced here: 57.6 us
  Pallas kernels  56.9 us (98%)
  between operations  0.64 us (1%)
    pallas_call x1, Pallas kernels, gather(): pl.pallas_call(functools.partial(gather_kernel, depth), out_shape=(jax.Sh...  50.2 us
    pallas_call x1, Pallas kernels, factor(): pl.pallas_call(factor_kernel, out_shape=(jax.ShapeDtypeStruct(sample.shap...  6.75 us

profile of v5, /device:TPU:1, one launch (start us, length us, event | category | flops | bytes accessed | tf_op | source)
XLA Modules:
  0.0 57.6 jit_solution(11392356692613824132)
XLA Ops:
  0.6 50.2 %gather.1 = (bf16[128,2048]{1,0:T(8,128)(2,1)}, f32[8,128,128]{2,1,0:T(8,128)}, f32[128,256]{1,0:T(8,128)}) custom-call(s32[8,8]{1,0:T(8,128)} %cols_ref.1, bf16[128,2048]{1,0:T(8,128)(2,1)} %probe_ref.1, bf16[8,8,256,256]{3,2,1,0:T(8,128)(2,1)} %blocks_ref.1), custom_call_target="tpu_custom_call" | custom-call | tf_op jit(solution)/shard_map/gather/pallas_call | solution.py:309
  50.8 6.8 %factor.1 = (bf16[128,2048]{1,0:T(8,128)(2,1)}, f32[8,128,128]{2,1,0:T(8,128)}, f32[1,128]{1,0:T(1,128)}) custom-call(f32[128,256]{1,0:T(8,128)} %get-tuple-element.6.c_ref, bf16[128,2048]{1,0:T(8,128)(2,1)} %get-tuple-element.7.sample_in, f32[8,128,128]{2,1,0:T(8,128)} %get-tuple-element.8.leaf_in), custom_call_target="tpu_custom_call" | custom-call | tf_op jit(solution)/shard_map/factor/pallas_call | solution.py:376

commit v6 on v5

--- a/solution.py
+++ b/solution.py
@@ -91,15 +91,31 @@
     layer, spot = row // PLANE, lax.rem(row, PLANE)
     side, front = lax.rem(spot, 4), spot // 4
 
+    ring = [0, 1, 2, 1]
+    plane_steps = sorted(
+        [(dx, dy) for dx in range(4) for dy in range(4) if dx or dy], key=lambda d: -ring[d[0]] - ring[d[1]]
+    )
+    column_steps = sorted(
+        [(dz, other) for dz in range(depth) for other in range(2) if dz or other],
+        key=lambda d: -2 * min(d[0], depth - d[0]) - d[1],
+    )
+    xs = [lax.rem(side + d, 4) for d in range(4)]
+    ys = [lax.rem(front + d, 4) for d in range(4)]
+    zs = [lax.rem(layer + d, depth) for d in range(depth)]
+    spots = {(dx, dy): ys[dy] * 4 + xs[dx] for dx in range(4) for dy in range(4)}
+
     def in_plane(step):
-        return (layer * PLANE + lax.rem(spot + step, PLANE), core)
+        return (layer * PLANE + spots[step], core)
 
     def in_column(step):
-        return (lax.rem(layer + step, depth) * PLANE + spot, lax.rem(core + step // depth, 2))
-
-    along_x = [(layer * PLANE + front * 4 + lax.rem(side + d, 4), core) for d in (1, 3)]
-    along_y = [in_plane(4), in_plane(12)]
-    along_z = [in_column(1), in_column(depth - 1)]
+        return (zs[step[0]] * PLANE + spot, 1 - core if step[1] else core)
+
+    def opposite(step):
+        return ((4 - step[0]) % 4, (4 - step[1]) % 4)
+
+    along_x = [in_plane((d, 0)) for d in (1, 3)]
+    along_y = [in_plane((0, d)) for d in (1, 3)]
+    along_z = [in_column((d, 0)) for d in (1, depth - 1)]
 
     def greet(semaphore, targets):
         for target in targets:
@@ -227,54 +243,64 @@
                 announce(t)
         if t >= 5:
             multiply(t - 5)
-        if t >= 6:
-            finish(t - 6)
-            if t < 8:
-                hand_out(t - 6)
+        if 6 <= t < 7:
+            finish(0)
+    finish(1)
+    finish(2)
     finish(3)
 
-    def scatter(step):
-        at = pl.multiple_of(lax.rem(spot + step, PLANE) * 8, 8)
-        return remote(total.at[pl.ds(at, 8), :], rs_buf.at[step], rs_send.at[step], rs_recv.at[step], in_plane(step))
-
-    def column(step):
-        return remote(z_buf.at[0], z_buf.at[step], z_send.at[step], z_recv.at[step], in_column(step))
-
     here = pl.ds(pl.multiple_of(spot * 8, 8), 8)
-
-    def publish(step):
-        return remote(root_ref.at[here, :], root_ref.at[here, :], ag_send.at[step], ag_recv.at[step], in_plane(step))
-
-    def published(step):
-        place = pl.ds(pl.multiple_of(lax.rem(spot + PLANE - step, PLANE) * 8, 8), 8)
-        return remote(root_ref.at[place, :], root_ref.at[place, :], ag_send.at[step], ag_recv.at[step], in_plane(step))
-
-    def each(count, act):
-        def body(step, carry):
-            act(step)
-            return carry
-
-        lax.fori_loop(1, count, body, 0)
-
-    each(PLANE, lambda step: scatter(step).start())
+    pieces = {step: pl.ds(pl.multiple_of(spots[step] * 8, 8), 8) for step in plane_steps}
+
+    scatters = [
+        remote(
+            total.at[pieces[step], :], rs_buf.at[step[1] * 4 + step[0]],
+            rs_send.at[step[1] * 4 + step[0]], rs_recv.at[step[1] * 4 + step[0]], in_plane(step),
+        )
+        for step in plane_steps
+    ]
+    for copy in scatters:
+        copy.start()
     rs_buf[0] = total[here, :]
-    hand_out(2)
-    hand_out(3)
+    for n in range(4):
+        hand_out(n)
     t0[...] = jnp.zeros_like(t0)
     t1[...] = jnp.zeros_like(t1)
     for k in range(0, 3):
         factor_panel(leaf_a, 4, t0, t1, k)
-    each(PLANE, lambda step: scatter(step).wait())
+    for copy in scatters:
+        copy.wait_recv()
     z_buf[0] = jnp.sum(rs_buf[...], axis=0)
-    each(2 * depth, lambda step: column(step).start())
+
+    columns = [
+        remote(
+            z_buf.at[0], z_buf.at[step[0] * 2 + step[1]],
+            z_send.at[step[0] * 2 + step[1]], z_recv.at[step[0] * 2 + step[1]], in_column(step),
+        )
+        for step in column_steps
+    ]
+    for copy in columns:
+        copy.start()
+    for copy in scatters:
+        copy.wait_send()
     for n in range(4):
         tiles[n].wait_recv()
         sample_out(4 + n, 7 - mine(n)).start()
     for k in range(3, 6):
         factor_panel(leaf_a, 4, t0, t1, k)
-    each(2 * depth, lambda step: column(step).wait())
+    for copy in columns:
+        copy.wait_recv()
     root_ref[here, :] = jnp.sum(z_buf[...], axis=0)
-    each(PLANE, lambda step: publish(step).start())
+
+    def publish(place, step):
+        at = step[1] * 4 + step[0]
+        return remote(root_ref.at[place, :], root_ref.at[place, :], ag_send.at[at], ag_recv.at[at], in_plane(step))
+
+    published = [publish(here, step) for step in plane_steps]
+    for copy in published:
+        copy.start()
+    for copy in columns:
+        copy.wait_send()
     for k in range(6, 8):
         factor_panel(leaf_a, 4, t0, t1, k)
     leaves = []
@@ -287,12 +313,10 @@
         leaves[n].wait_recv()
     leaf_out = pltpu.make_async_copy(leaf_buf, leaf_ref, leaf_sem)
     leaf_out.start()
-
-    def close(step):
-        publish(step).wait_send()
-        published(step).wait_recv()
-
-    each(PLANE, close)
+    for copy in published:
+        copy.wait_send()
+    for step in plane_steps:
+        publish(pieces[opposite(step)], step).wait_recv()
     share.wait_send()
     for copy in list(halo.values()) + list(passed.values()) + list(parts.values()) + list(tiles.values()) + leaves:
         copy.wait_send()

time: 57.8 us -> 56.6 us (0.979)
  Pallas kernels: 56.9 us -> 55.7 us
    pallas_call x1, Pallas kernels: 50.2 us -> 49 us  [gather(): pl.pallas_call(functools.partial(gather_kernel, depth), out_shape=(jax.Sh...]
where the time goes in v6:
time: 56.6 us; the launch traced here: 56.4 us
  Pallas kernels  55.7 us (98%)
  between operations  0.64 us (1%)
    pallas_call x1, Pallas kernels, gather(): pl.pallas_call(functools.partial(gather_kernel, depth), out_shape=(jax.Sh...  49 us
    pallas_call x1, Pallas kernels, factor(): pl.pallas_call(factor_kernel, out_shape=(jax.ShapeDtypeStruct(sample.shap...  6.75 us

profile of v6, /device:TPU:1, one launch (start us, length us, event | category | flops | bytes accessed | tf_op | source)
XLA Modules:
  0.0 56.4 jit_solution(2696643162906170256)
XLA Ops:
  0.6 49.0 %gather.1 = (bf16[128,2048]{1,0:T(8,128)(2,1)}, f32[8,128,128]{2,1,0:T(8,128)}, f32[128,256]{1,0:T(8,128)}) custom-call(s32[8,8]{1,0:T(8,128)} %cols_ref.1, bf16[128,2048]{1,0:T(8,128)(2,1)} %probe_ref.1, bf16[8,8,256,256]{3,2,1,0:T(8,128)(2,1)} %blocks_ref.1), custom_call_target="tpu_custom_call" | custom-call | tf_op jit(solution)/shard_map/gather/pallas_call | solution.py:333
  49.6 6.8 %factor.1 = (bf16[128,2048]{1,0:T(8,128)(2,1)}, f32[8,128,128]{2,1,0:T(8,128)}, f32[1,128]{1,0:T(1,128)}) custom-call(f32[128,256]{1,0:T(8,128)} %get-tuple-element.6.c_ref, bf16[128,2048]{1,0:T(8,128)(2,1)} %get-tuple-element.7.sample_in, f32[8,128,128]{2,1,0:T(8,128)} %get-tuple-element.8.leaf_in), custom_call_target="tpu_custom_call" | custom-call | tf_op jit(solution)/shard_map/factor/pallas_call | solution.py:400

commit v7 on v6

--- a/solution.py
+++ b/solution.py
@@ -93,29 +93,38 @@
 
     ring = [0, 1, 2, 1]
     plane_steps = sorted(
-        [(dx, dy) for dx in range(4) for dy in range(4) if dx or dy], key=lambda d: -ring[d[0]] - ring[d[1]]
+        [(dx, dy, o) for dx in range(4) for dy in range(4) for o in range(2) if dx or dy or o],
+        key=lambda d: -ring[d[0]] - ring[d[1]],
     )
-    column_steps = sorted(
-        [(dz, other) for dz in range(depth) for other in range(2) if dz or other],
-        key=lambda d: -2 * min(d[0], depth - d[0]) - d[1],
-    )
+    column_steps = sorted(range(1, depth), key=lambda d: -min(d, depth - d))
     xs = [lax.rem(side + d, 4) for d in range(4)]
     ys = [lax.rem(front + d, 4) for d in range(4)]
     zs = [lax.rem(layer + d, depth) for d in range(depth)]
     spots = {(dx, dy): ys[dy] * 4 + xs[dx] for dx in range(4) for dy in range(4)}
 
+    cores = (core, 1 - core)
+
     def in_plane(step):
-        return (layer * PLANE + spots[step], core)
+        return (layer * PLANE + spots[step[:2]], cores[step[2]])
 
     def in_column(step):
-        return (zs[step[0]] * PLANE + spot, 1 - core if step[1] else core)
+        return (zs[step] * PLANE + spot, core)
 
     def opposite(step):
-        return ((4 - step[0]) % 4, (4 - step[1]) % 4)
-
-    along_x = [in_plane((d, 0)) for d in (1, 3)]
-    along_y = [in_plane((0, d)) for d in (1, 3)]
-    along_z = [in_column((d, 0)) for d in (1, depth - 1)]
+        return ((4 - step[0]) % 4, (4 - step[1]) % 4, step[2])
+
+    def tile(step):
+        return (
+            pl.ds(pl.multiple_of(spots[step[:2]] * 8, 8), 8),
+            pl.ds(pl.multiple_of(cores[step[2]] * K, K), K),
+        )
+
+    def slot(step):
+        return (step[1] * 4 + step[0]) * 2 + step[2]
+
+    along_x = [in_plane((d, 0, 0)) for d in (1, 3)]
+    along_y = [in_plane((0, d, 0)) for d in (1, 3)]
+    along_z = [in_column(d) for d in (1, depth - 1)]
 
     def greet(semaphore, targets):
         for target in targets:
@@ -249,19 +258,14 @@
     finish(2)
     finish(3)
 
-    here = pl.ds(pl.multiple_of(spot * 8, 8), 8)
-    pieces = {step: pl.ds(pl.multiple_of(spots[step] * 8, 8), 8) for step in plane_steps}
-
+    here = tile((0, 0, 0))
     scatters = [
-        remote(
-            total.at[pieces[step], :], rs_buf.at[step[1] * 4 + step[0]],
-            rs_send.at[step[1] * 4 + step[0]], rs_recv.at[step[1] * 4 + step[0]], in_plane(step),
-        )
+        remote(total.at[tile(step)], rs_buf.at[slot(step)], rs_send.at[slot(step)], rs_recv.at[slot(step)], in_plane(step))
         for step in plane_steps
     ]
     for copy in scatters:
         copy.start()
-    rs_buf[0] = total[here, :]
+    rs_buf[0] = total[here]
     for n in range(4):
         hand_out(n)
     t0[...] = jnp.zeros_like(t0)
@@ -273,10 +277,7 @@
     z_buf[0] = jnp.sum(rs_buf[...], axis=0)
 
     columns = [
-        remote(
-            z_buf.at[0], z_buf.at[step[0] * 2 + step[1]],
-            z_send.at[step[0] * 2 + step[1]], z_recv.at[step[0] * 2 + step[1]], in_column(step),
-        )
+        remote(z_buf.at[0], z_buf.at[step], z_send.at[step], z_recv.at[step], in_column(step))
         for step in column_steps
     ]
     for copy in columns:
@@ -290,11 +291,11 @@
         factor_panel(leaf_a, 4, t0, t1, k)
     for copy in columns:
         copy.wait_recv()
-    root_ref[here, :] = jnp.sum(z_buf[...], axis=0)
+    root_ref[here] = jnp.sum(z_buf[...], axis=0)
 
     def publish(place, step):
-        at = step[1] * 4 + step[0]
-        return remote(root_ref.at[place, :], root_ref.at[place, :], ag_send.at[at], ag_recv.at[at], in_plane(step))
+        at = slot(step)
+        return remote(root_ref.at[place], root_ref.at[place], ag_send.at[at], ag_recv.at[at], in_plane(step))
 
     published = [publish(here, step) for step in plane_steps]
     for copy in published:
@@ -316,7 +317,7 @@
     for copy in published:
         copy.wait_send()
     for step in plane_steps:
-        publish(pieces[opposite(step)], step).wait_recv()
+        publish(tile(opposite(step)), step).wait_recv()
     share.wait_send()
     for copy in list(halo.values()) + list(passed.values()) + list(parts.values()) + list(tiles.values()) + leaves:
         copy.wait_send()
@@ -350,8 +351,8 @@
             pltpu.VMEM((8, K, LEAF), bf16),
             pltpu.VMEM((4, K, LEAF), bf16),
             pltpu.VMEM((K, LEAF), f32),
-            pltpu.VMEM((PLANE, 8, LEAF), f32),
-            pltpu.VMEM((2 * depth, 8, LEAF), f32),
+            pltpu.VMEM((2 * PLANE, 8, K), f32),
+            pltpu.VMEM((depth, 8, K), f32),
             pltpu.VMEM((4, K, 2 * K), f32),
             pltpu.VMEM((PANEL * SUB, K), f32),
             pltpu.VMEM((PANEL * SUB, K), f32),
@@ -360,7 +361,7 @@
             pltpu.SemaphoreType.REGULAR((7,)),
             dma((8,)), dma((8,)), dma, dma, dma((2, 8)), dma((2, 8)), dma((2, 8)), dma((2, 8)),
             dma((4,)), dma((4,)), dma((4,)), dma((4,)), dma((8,)), dma((4,)), dma((4,)), dma,
-            dma((PLANE,)), dma((PLANE,)), dma((2 * depth,)), dma((2 * depth,)), dma((PLANE,)), dma((PLANE,)),
+            dma((2 * PLANE,)), dma((2 * PLANE,)), dma((depth,)), dma((depth,)), dma((2 * PLANE,)), dma((2 * PLANE,)),
         ],
         compiler_params=pltpu.CompilerParams(
             collective_id=0, has_side_effects=True, vmem_limit_bytes=56 * 2**20

time: 56.6 us -> 57.2 us (1.011)
  Pallas kernels: 55.7 us -> 56.3 us
    pallas_call x1, Pallas kernels: 49 us -> 49.6 us  [gather(): pl.pallas_call(functools.partial(gather_kernel, depth), out_shape=(jax.Sh...]
where the time goes in v7:
time: 57.2 us; the launch traced here: 57 us
  Pallas kernels  56.3 us (98%)
  between operations  0.64 us (1%)
    pallas_call x1, Pallas kernels, gather(): pl.pallas_call(functools.partial(gather_kernel, depth), out_shape=(jax.Sh...  49.6 us
    pallas_call x1, Pallas kernels, factor(): pl.pallas_call(factor_kernel, out_shape=(jax.ShapeDtypeStruct(sample.shap...  6.75 us

profile of v7, /device:TPU:1, one launch (start us, length us, event | category | flops | bytes accessed | tf_op | source)
XLA Modules:
  0.0 57.0 jit_solution(8211397709552578759)
XLA Ops:
  0.6 49.6 %gather.1 = (bf16[128,2048]{1,0:T(8,128)(2,1)}, f32[8,128,128]{2,1,0:T(8,128)}, f32[128,256]{1,0:T(8,128)}) custom-call(s32[8,8]{1,0:T(8,128)} %cols_ref.1, bf16[128,2048]{1,0:T(8,128)(2,1)} %probe_ref.1, bf16[8,8,256,256]{3,2,1,0:T(8,128)(2,1)} %blocks_ref.1), custom_call_target="tpu_custom_call" | custom-call | tf_op jit(solution)/shard_map/gather/pallas_call | solution.py:334
  50.2 6.8 %factor.1 = (bf16[128,2048]{1,0:T(8,128)(2,1)}, f32[8,128,128]{2,1,0:T(8,128)}, f32[1,128]{1,0:T(1,128)}) custom-call(f32[128,256]{1,0:T(8,128)} %get-tuple-element.6.c_ref, bf16[128,2048]{1,0:T(8,128)(2,1)} %get-tuple-element.7.sample_in, f32[8,128,128]{2,1,0:T(8,128)} %get-tuple-element.8.leaf_in), custom_call_target="tpu_custom_call" | custom-call | tf_op jit(solution)/shard_map/factor/pallas_call | solution.py:401

commit v8 on v6

--- a/solution.py
+++ b/solution.py
@@ -133,6 +133,7 @@
             probe_ref.at[:, c * LEAF:(c + 1) * LEAF], own.at[core, c], own_sem.at[c]
         )
         own_copies[c].start()
+    root_ref[...] = jnp.zeros_like(root_ref)
     barrier = pltpu.get_barrier_semaphore()
     entered = [after, before, sibling] + along_x + along_y + along_z
     greet(barrier, entered)
@@ -292,13 +293,26 @@
         copy.wait_recv()
     root_ref[here, :] = jnp.sum(z_buf[...], axis=0)
 
-    def publish(place, step):
+    def publish(place, step, width):
         at = step[1] * 4 + step[0]
-        return remote(root_ref.at[place, :], root_ref.at[place, :], ag_send.at[at], ag_recv.at[at], in_plane(step))
-
-    published = [publish(here, step) for step in plane_steps]
-    for copy in published:
-        copy.start()
+        part = root_ref.at[place, 0:width]
+        return remote(part, part, ag_send.at[at], ag_recv.at[at], in_plane(step))
+
+    upper = layer * (2 * PLANE) >= K
+    widths = ((LEAF, upper), (K, jnp.logical_not(upper)))
+
+    def start_publishing(width):
+        for step in plane_steps:
+            publish(here, step, width).start()
+
+    def end_publishing(width):
+        for step in plane_steps:
+            publish(here, step, width).wait_send()
+        for step in plane_steps:
+            publish(pieces[opposite(step)], step, width).wait_recv()
+
+    for width, when in widths:
+        pl.when(when)(functools.partial(start_publishing, width))
     for copy in columns:
         copy.wait_send()
     for k in range(6, 8):
@@ -313,10 +327,8 @@
         leaves[n].wait_recv()
     leaf_out = pltpu.make_async_copy(leaf_buf, leaf_ref, leaf_sem)
     leaf_out.start()
-    for copy in published:
-        copy.wait_send()
-    for step in plane_steps:
-        publish(pieces[opposite(step)], step).wait_recv()
+    for width, when in widths:
+        pl.when(when)(functools.partial(end_publishing, width))
     share.wait_send()
     for copy in list(halo.values()) + list(passed.values()) + list(parts.values()) + list(tiles.values()) + leaves:
         copy.wait_send()

time: 56.6 us -> 56.3 us (level)
  no operation moved by 1% of the time
where the time goes in v8:
time: 56.3 us; the launch traced here: 56.2 us
  Pallas kernels  55.5 us (99%)
  between operations  0.64 us (1%)
    pallas_call x1, Pallas kernels, gather(): pl.pallas_call(functools.partial(gather_kernel, depth), out_shape=(jax.Sh...  48.8 us
    pallas_call x1, Pallas kernels, factor(): pl.pallas_call(factor_kernel, out_shape=(jax.ShapeDtypeStruct(sample.shap...  6.75 us

profile of v8, /device:TPU:1, one launch (start us, length us, event | category | flops | bytes accessed | tf_op | source)
XLA Modules:
  0.0 56.2 jit_solution(12174114361851025638)
XLA Ops:
  0.6 48.8 %gather.1 = (bf16[128,2048]{1,0:T(8,128)(2,1)}, f32[8,128,128]{2,1,0:T(8,128)}, f32[128,256]{1,0:T(8,128)}) custom-call(s32[8,8]{1,0:T(8,128)} %cols_ref.1, bf16[128,2048]{1,0:T(8,128)(2,1)} %probe_ref.1, bf16[8,8,256,256]{3,2,1,0:T(8,128)(2,1)} %blocks_ref.1), custom_call_target="tpu_custom_call" | custom-call | tf_op jit(solution)/shard_map/gather/pallas_call | solution.py:345
  49.4 6.8 %factor.1 = (bf16[128,2048]{1,0:T(8,128)(2,1)}, f32[8,128,128]{2,1,0:T(8,128)}, f32[1,128]{1,0:T(1,128)}) custom-call(f32[128,256]{1,0:T(8,128)} %get-tuple-element.6.c_ref, bf16[128,2048]{1,0:T(8,128)(2,1)} %get-tuple-element.7.sample_in, f32[8,128,128]{2,1,0:T(8,128)} %get-tuple-element.8.leaf_in), custom_call_target="tpu_custom_call" | custom-call | tf_op jit(solution)/shard_map/factor/pallas_call | solution.py:412
